TPU v7x, 128 devices: a whole 4x4x4 slice. The times are simulated.
128 devices in a mesh: rep: 2 (over x_hi), row: 8 (over y, core), col: 8 (over x_lo, z).
Axes of the slice: x: 4 (x_hi: 2, x_lo: 2; x = x_hi * 2 + x_lo), y: 4, z: 4, core: 2. Of those that a mesh axis runs over, the one named last changes fastest.
Arguments:
- replica_deltas: bfloat16 [2, 4096, 4096], P('rep', 'row', 'col'), may hold values from -8 to 8
- weights: float32 [4096, 4096], P('row', 'col'), may hold values from -6 to 6
- momentum: float32 [4096, 4096], P('row', 'col'), may hold values from -6 to 6
- left_state: float32 [4096, 4096], P('row', ('rep', 'col')), may hold values from -0.5 to 4.5
- right_state: float32 [4096, 4096], P(('rep', 'row'), 'col'), may hold values from -0.5 to 4.5
- left_root: bfloat16 [4096, 4096], P('row', ('rep', 'col')), may hold values from -0.5 to 2.5
- right_root: bfloat16 [4096, 4096], P(('rep', 'row'), 'col'), may hold values from -0.5 to 2.5
Outputs:
- new_weights: float32 [4096, 4096], P('row', 'col')
- new_momentum: float32 [4096, 4096], P('row', 'col')
- new_left: float32 [4096, 4096], P('row', ('rep', 'col'))
- new_right: float32 [4096, 4096], P(('rep', 'row'), 'col')
All inputs are finite; a program needn't handle non-finite values.
Results may differ from a plain program's by a relative error of at most 0.0054.
Values may be sent and summed in bfloat16 or wider, within the bound.
A program may use at most 128 MiB of HBM per device.

v0:
```python
import jax
import jax.numpy as jnp
from jax import lax
from jax.sharding import PartitionSpec as P

decay_rate = 0.9
momentum_rate = 0.9
outer_rate = 0.7
contract_last = (((1,), (1,)), ((), ()))
contract_first = (((0,), (0,)), ((), ()))


def shards(replica_deltas, weights, momentum, left_state, right_state, left_root, right_root):
    replicas = lax.axis_size("rep")
    replica = lax.axis_index("rep")
    summed = lax.psum(replica_deltas[0].astype(jnp.float32).astype(jnp.bfloat16), "rep").astype(
        jnp.float32
    )
    grad = (summed / replicas).astype(jnp.bfloat16)
    tile_rows = grad.shape[0]
    tile_cols = grad.shape[1]
    row_band = lax.all_gather(grad, "col", axis=1, tiled=True)
    total_cols = row_band.shape[1]
    half_cols = tile_cols // replicas
    mine_cols = lax.dynamic_slice_in_dim(grad, replica * half_cols, half_cols, 1)
    col_band = lax.all_gather(mine_cols, "row", axis=0, tiled=True)
    total_rows = col_band.shape[0]
    block = col_band
    left_sum = lax.psum_scatter(
        lax.dot_general(block, mine_cols, contract_last, preferred_element_type=jnp.float32).astype(
            jnp.bfloat16
        ),
        ("rep", "col"),
        scatter_dimension=0,
        tiled=True,
    ).astype(jnp.float32)
    half_rows = tile_rows // replicas
    band_rows = lax.dynamic_slice_in_dim(row_band, replica * half_rows, half_rows, 0)
    mine_rows = lax.dynamic_slice_in_dim(grad, replica * half_rows, half_rows, 0)
    block = band_rows
    right_sum = lax.psum_scatter(
        lax.dot_general(
            block, mine_rows, contract_first, preferred_element_type=jnp.float32
        ).astype(jnp.bfloat16),
        ("rep", "row"),
        scatter_dimension=0,
        tiled=True,
    ).astype(jnp.float32)
    left_gram = left_sum.T
    new_left = decay_rate * left_state + (1.0 - decay_rate) / total_cols * left_gram
    new_right = decay_rate * right_state + (1.0 - decay_rate) / total_rows * right_sum
    block = row_band
    mixed = jnp.dot(
        block,
        lax.all_gather(right_root, ("rep", "row"), axis=0, tiled=True),
        preferred_element_type=jnp.float32,
    )
    mixed = mixed.astype(jnp.bfloat16)
    left_band = lax.all_gather(left_root, ("rep", "col"), axis=1, tiled=True)
    block = left_band
    update = jnp.dot(
        block, lax.all_gather(mixed, "row", axis=0, tiled=True), preferred_element_type=jnp.float32
    )
    new_momentum = momentum_rate * momentum + update
    new_weights = weights - outer_rate * (momentum_rate * new_momentum + update)
    return (new_weights, new_momentum, new_left, new_right)


def solution(mesh):
    in_specs = (
        P("rep", "row", "col"),
        P("row", "col"),
        P("row", "col"),
        P("row", ("rep", "col")),
        P(("rep", "row"), "col"),
        P("row", ("rep", "col")),
        P(("rep", "row"), "col"),
    )
    out_specs = (
        P("row", "col"),
        P("row", "col"),
        P("row", ("rep", "col")),
        P(("rep", "row"), "col"),
    )
    return jax.shard_map(shards, mesh=mesh, in_specs=in_specs, out_specs=out_specs, check_vma=False)
```

profile of v0, /device:TPU:0, one launch (start us, length us, event | category | flops | bytes accessed | tf_op | source)
XLA Modules:
  0.0 459.6 jit_solution(7989351003090285797)
XLA Ops:
  7.2 0.0 all-reduce.2.cloned.1.call-start
  7.2 0.7 all-reduce.2.cloned.1.call-update
  7.9 0.0 all-gather.14.cloned.1.call-start
  7.9 41.7 %all-reduce.2.cloned.1.call-done = bf16[512,512]{1,0:T(8,128)(2,1)} async-done(((bf16[512,512]{1,0:T(8,128)(2,1)}), bf16[512,512]{1,0:T(8,128)(2,1)}) %all-reduce.2.cloned.1.call-update) | async-done | bytes 524304 | tf_op jit(solution)/shard_map/psum | solution.py:16
  49.6 1.1 multiply_convert_fusion
  50.7 0.0 copy-start
  50.7 0.8 constant_dynamic-slice_fusion
  51.5 0.0 all-gather.14.cloned.1.call-update
  51.6 0.0 all-gather.6.cloned.1.call-start
  51.6 0.0 copy-done
  51.6 0.7 all-gather.6.cloned.1.call-update
  52.3 0.0 all-gather.8.cloned.1.call-start
  52.4 0.5 all-gather.8.cloned.1.call-update
  52.9 0.0 reduce-scatter.3.cloned.1.call-start
  52.9 23.7 %all-gather.14.cloned.1.call-done = bf16[4096,256]{1,0:T(8,128)(2,1)} async-done(((bf16[512,256]{1,0:T(8,128)(2,1)}), bf16[4096,256]{1,0:T(8,128)(2,1)}) %all-gather.14.cloned.1.call-update) | async-done | bytes 2097168 | tf_op jit(solution)/shard_map/all_gather | solution.py:26
  76.7 4.9 %convolution_convert_fusion.1 = bf16[4096,512]{1,0:T(8,128)(2,1)} fusion(bf16[4096,256]{1,0:T(8,128)(2,1)} %all-gather.14.cloned.1.call-done, bf16[512,256]{1,0:T(8,128)(2,1)} %constant_dynamic-slice_fusion), kind=kOutput, calls=%fused_computation.1 | convolution fusion | flops 1075838976 | bytes 6553600 | tf_op jit(solution)/shard_map/dot_general | solution.py:30
  81.6 0.0 copy-start.1
  81.6 0.0 reduce-scatter.3.cloned.1.call-update
  81.6 0.0 reduce-scatter.5.cloned.1.call-start
  81.6 50.5 %all-gather.6.cloned.1.call-done = bf16[512,4096]{1,0:T(8,128)(2,1)} async-done(((bf16[512,512]{1,0:T(8,128)(2,1)}), bf16[512,4096]{1,0:T(8,128)(2,1)}) %all-gather.6.cloned.1.call-update) | async-done | bytes 4194320 | tf_op jit(solution)/shard_map/all_gather | solution.py:22
  132.1 0.0 copy-done.1
  132.1 4.8 %convolution_convert_fusion = bf16[4096,512]{1,0:T(8,128)(2,1)} fusion(bf16[512,4096]{1,0:T(8,128)(2,1)} %all-gather.6.cloned.1.call-done, s32[]{:T(128)S(6)} %select_n.2, bf16[512,512]{1,0:T(8,128)(2,1)S(1)} %copy-done.1), kind=kOutput, calls=%fused_computation | convolution fusion | flops 1075838976 | bytes 6554624 | tf_op jit(solution)/shard_map/dot_general | solution.py:42
  136.9 0.0 reduce-scatter.5.cloned.1.call-update
  137.0 0.0 all-gather.12.cloned.1.call-start
  137.0 0.7 all-gather.12.cloned.1.call-update
  137.7 0.0 copy-start.4
  137.7 0.0 copy-start.2
  137.7 0.0 all-gather.10.cloned.1.call-start
  137.8 50.8 %all-gather.8.cloned.1.call-done = bf16[4096,512]{1,0:T(8,128)(2,1)} async-done(((bf16[256,512]{1,0:T(8,128)(2,1)}), bf16[4096,512]{1,0:T(8,128)(2,1)}) %all-gather.8.cloned.1.call-update) | async-done | bytes 4194320 | tf_op jit(solution)/shard_map/all_gather | solution.py:55
  188.6 6.6 %convolution_convert_fusion.2 = bf16[512,512]{1,0:T(8,128)(2,1)} fusion(bf16[512,4096]{1,0:T(8,128)(2,1)} %all-gather.6.cloned.1.call-done, bf16[4096,512]{1,0:T(8,128)(2,1)} %all-gather.8.cloned.1.call-done), kind=kOutput, calls=%fused_computation.4 | convolution fusion | flops 2147745792 | bytes 8912896 | tf_op jit(solution)/shard_map/dot_general | solution.py:53
  195.2 0.0 copy-start.3
  195.2 0.0 all-gather.10.cloned.1.call-update
  195.2 0.0 copy-done.4
  195.2 0.2 copy.13
  195.4 0.0 copy-done.2
  195.4 0.0 copy-start.5
  195.4 1.3 copy.11
  196.7 0.0 copy-done.3
  196.7 1.3 copy.12
  198.1 69.8 %reduce-scatter.3.cloned.1.call-done = bf16[256,512]{1,0:T(8,128)(2,1)} async-done(((bf16[4096,512]{1,0:T(8,128)(2,1)}), bf16[256,512]{1,0:T(8,128)(2,1)}) %reduce-scatter.3.cloned.1.call-update) | async-done | bytes 262160 | tf_op jit(solution)/shard_map/reduce_scatter | solution.py:29
  267.9 1.0 bitcast_add_fusion
  268.9 1.0 copy.16
  269.9 81.6 %reduce-scatter.5.cloned.1.call-done = bf16[256,512]{1,0:T(8,128)(2,1)} async-done(((bf16[4096,512]{1,0:T(8,128)(2,1)}), bf16[256,512]{1,0:T(8,128)(2,1)}) %reduce-scatter.5.cloned.1.call-update) | async-done | bytes 262160 | tf_op jit(solution)/shard_map/reduce_scatter | solution.py:41
  351.5 0.0 copy-done.5
  351.5 1.8 multiply_add_fusion.1
  353.3 57.1 %all-gather.12.cloned.1.call-done = bf16[512,4096]{1,0:T(8,128)(2,1)} async-done(((bf16[512,256]{1,0:T(8,128)(2,1)}), bf16[512,4096]{1,0:T(8,128)(2,1)}) %all-gather.12.cloned.1.call-update) | async-done | bytes 4194320 | tf_op jit(solution)/shard_map/all_gather | solution.py:59
  410.4 33.3 %all-gather.10.cloned.1.call-done = bf16[4096,512]{1,0:T(8,128)(2,1)} async-done(((bf16[512,512]{1,0:T(8,128)(2,1)}), bf16[4096,512]{1,0:T(8,128)(2,1)}) %all-gather.10.cloned.1.call-update) | async-done | bytes 4194320 | tf_op jit(solution)/shard_map/all_gather | solution.py:62
  443.7 6.5 %multiply_add_fusion = (f32[512,512]{0,1:T(8,128)S(1)}, f32[512,512]{0,1:T(8,128)S(1)}) fusion(f32[512,512]{0,1:T(8,128)} %copy.11, f32[512,512]{0,1:T(8,128)} %copy.12, bf16[4096,512]{1,0:T(8,128)(2,1)} %all-gather.10.cloned.1.call-done, bf16[512,4096]{1,0:T(8,128)(2,1)} %all-gather.12.cloned.1.call-done), kind=kOutput, calls=%fused_computation.7 | convolution fusion | flops 2149056512 | bytes 12582912 | tf_op jit(solution)/shard_map/dot_general | solution.py:61
  450.1 1.3 copy.14
  451.5 1.3 copy.15
Async XLA Ops:
  7.2 42.4 %all-reduce.2.cloned.1.call-start = ((), (), s32[]{:S(2)}) async-start(), calls=%async_computation.2 | async-start | bytes 1048576 | tf_op jit(solution)/shard_map/psum | solution.py:16
  7.9 68.8 %all-gather.14.cloned.1.call-start = ((), (), s32[]{:S(2)}) async-start(), calls=%async_computation.7 | async-start | bytes 2359296 | tf_op jit(solution)/shard_map/all_gather | solution.py:26
  50.7 0.9 copy-start
  51.6 80.5 %all-gather.6.cloned.1.call-start = ((), (), s32[]{:S(2)}) async-start(), calls=%async_computation.3 | async-start | bytes 4718592 | tf_op jit(solution)/shard_map/all_gather | solution.py:22
  52.3 136.3 %all-gather.8.cloned.1.call-start = ((), (), s32[]{:S(2)}) async-start(), calls=%async_computation.4 | async-start | bytes 4456448 | tf_op jit(solution)/shard_map/all_gather | solution.py:55
  52.9 215.0 %reduce-scatter.3.cloned.1.call-start = ((), (), s32[]{:S(2)}) async-start(), calls=%async_computation.8 | async-start | bytes 4456448 | tf_op jit(solution)/shard_map/reduce_scatter | solution.py:29
  81.6 50.6 %copy-start.1 = (bf16[512,512]{1,0:T(8,128)(2,1)S(1)}, bf16[512,512]{1,0:T(8,128)(2,1)}, u32[]{:S(2)}) copy-start(bf16[512,512]{1,0:T(8,128)(2,1)} %copy-done) | copy-start | bytes 1572868
  81.6 269.9 %reduce-scatter.5.cloned.1.call-start = ((), (), s32[]{:S(2)}) async-start(), calls=%async_computation.9 | async-start | bytes 4456448 | tf_op jit(solution)/shard_map/reduce_scatter | solution.py:41
  137.0 273.5 %all-gather.12.cloned.1.call-start = ((), (), s32[]{:S(2)}) async-start(), calls=%async_computation.6 | async-start | bytes 4456448 | tf_op jit(solution)/shard_map/all_gather | solution.py:59
  137.7 57.5 %copy-start.4 = (f32[512,256]{1,0:T(8,128)S(1)}, f32[512,256]{1,0:T(8,128)}, u32[]{:S(2)}) copy-start(f32[512,256]{1,0:T(8,128)} %param.10) | copy-start | bytes 1572868
  137.7 57.7 %copy-start.2 = (f32[512,512]{1,0:T(8,128)S(1)}, f32[512,512]{1,0:T(8,128)}, u32[]{:S(2)}) copy-start(f32[512,512]{1,0:T(8,128)} %param.9) | copy-start | bytes 3145732
  137.7 305.9 %all-gather.10.cloned.1.call-start = ((), (), s32[]{:S(2)}) async-start(), calls=%async_computation.5 | async-start | bytes 4718592 | tf_op jit(solution)/shard_map/all_gather | solution.py:62
  195.2 1.6 copy-start.3
  195.4 156.1 %copy-start.5 = (f32[256,512]{1,0:T(8,128)S(1)}, f32[256,512]{1,0:T(8,128)}, u32[]{:S(2)}) copy-start(f32[256,512]{1,0:T(8,128)} %param.11) | copy-start | bytes 1572868
Sparse Core Ops, SparseCore 0:
  10.4 39.1 all-reduce.1
  52.0 24.6 all-gather.13
  79.0 53.0 all-gather.5
  134.7 53.7 all-gather.7
  192.1 75.7 reduce-scatter.2
  271.7 79.7 reduce-scatter.4
  353.8 56.5 all-gather.11
  412.2 31.3 all-gather.9
where the time goes:
time: 461 us; the launch traced here: 460 us
  waiting for transfers between devices  411 us (89%)
  matrix products  22.8 us (5%)
  between operations  14.2 us (3%)
  local copies, waits for them, and re-layouts  7.25 us (2%)
    reduce_scatter x1, waiting for transfers between devices, shards(): lax.psum_scatter(lax.dot_general(block, mine_rows, contract_first, prefer...  81.6 us
    reduce_scatter x1, waiting for transfers between devices, shards(): lax.psum_scatter(lax.dot_general(block, mine_cols, contract_last, preferr...  69.8 us
    all_gather x1, waiting for transfers between devices, shards(): left_band = lax.all_gather(left_root, ('rep', 'col'), axis=1, tiled=True)  57.1 us
    all_gather x1, waiting for transfers between devices, shards(): lax.all_gather(right_root, ('rep', 'row'), axis=0, tiled=True)  50.8 us
    all_gather x1, waiting for transfers between devices, shards(): row_band = lax.all_gather(grad, 'col', axis=1, tiled=True)  50.5 us
    psum x1, waiting for transfers between devices, shards(): lax.psum(replica_deltas[0].astype(jnp.float32).astype(jnp.bfloat16), 'rep')  41.7 us
    all_gather x1, waiting for transfers between devices, shards(): lax.all_gather(mixed, 'row', axis=0, tiled=True)  33.3 us
    all_gather x1, waiting for transfers between devices, shards(): col_band = lax.all_gather(mine_cols, 'row', axis=0, tiled=True)  23.7 us
  transfers between devices with their start and end apart: 8, of which 8 were waited for; matrix products, arithmetic and copies ran while one was open for 5% of the time, Pallas kernels for 0%

commit v1 on v0

v1 whole, which is shorter than its diff:
```python
import functools

import jax
import jax.numpy as jnp
from jax import lax
from jax.experimental import pallas as pl
from jax.experimental.pallas import tpu as pltpu
from jax.sharding import PartitionSpec as P

decay_rate = 0.9
momentum_rate = 0.9
outer_rate = 0.7

MESH = pl.DeviceIdType.MESH
ORDER = (1, 3, 2)
HALF = 256
FULL = 512
SPLIT = 256
N_COPIES = 85


def lanes(chunk):
    return pl.ds(pl.multiple_of(chunk * HALF, HALF), HALF)


def rows_at(chunk, size):
    return pl.ds(pl.multiple_of(chunk * size, size), size)


def nn(a, b):
    return jnp.dot(a, b, preferred_element_type=jnp.float32)


def nt(a, b):
    return lax.dot_general(a, b, (((1,), (1,)), ((), ())), preferred_element_type=jnp.float32)


def tn(a, b):
    return lax.dot_general(a, b, (((0,), (0,)), ((), ())), preferred_element_type=jnp.float32)


def kernel(
    delta, left_root, right_root,
    out_pre, out_left, out_right,
    d_own, d_in, g_row, l_row, r_col, m_col, l_band,
    q_out, q_own, q_in, s_out, s_in, p_out, p_in,
    local_sem, send_sem, recv_sem,
):
    rep = lax.axis_index("rep")
    row = lax.axis_index("row")
    col = lax.axis_index("col")
    x, y, z, h = rep * 2 + col // 4, row // 2, col % 4, row % 2
    xl = col // 4

    def dev(xx, yy, zz, hh):
        return (xx // 2, yy * 2 + hh, (xx % 2) * 4 + zz)

    def along_x(d):
        return dev((x + d) % 4, y, z, h)

    def along_y(d):
        return dev(x, (y + d) % 4, z, h)

    def along_z(d):
        return dev(x, y, (z + d) % 4, h)

    mate = dev(x, y, z, 1 - h)
    twin = along_x(2)
    turned = [dev(y, x, 2 * h + i, 1 - z // 2) for i in range(2)]
    turned_from = [dev(y, x, 2 * (1 - h) + i, z // 2) for i in range(2)]

    copies = []

    def send(src, dst, device, slot=None):
        i = len(copies)
        cp = pltpu.make_async_remote_copy(
            src_ref=src, dst_ref=dst, send_sem=send_sem.at[i],
            recv_sem=recv_sem.at[i if slot is None else slot],
            device_id=device, device_id_type=MESH,
        )
        cp.start()
        copies.append(cp)
        return cp

    own_g = lanes(4 * z + x)
    own_l = lanes(4 * x + z)
    own_r = rows_at(4 * y + 2 * h + rep, HALF)
    load_l = pltpu.make_async_copy(left_root, l_row.at[:, own_l], local_sem.at[0])
    load_d = pltpu.make_async_copy(delta.at[:, lanes(rep)], d_own, local_sem.at[1])
    load_r = pltpu.make_async_copy(right_root.at[:, lanes(rep)], r_col.at[own_r], local_sem.at[2])
    load_d.start()
    load_l.start()
    load_r.start()

    barrier = pltpu.get_barrier_semaphore()
    partners = [f(d) for f in (along_x, along_y, along_z) for d in ORDER] + [mate] + turned + turned_from
    for partner in partners:
        pl.semaphore_signal(barrier, inc=1, device_id=partner, device_id_type=MESH)
    pl.semaphore_wait(barrier, len(partners))

    d_swap = send(delta.at[:, lanes(1 - rep)], d_in, twin)
    r_swap = send(right_root.at[:, lanes(1 - rep)], r_col.at[own_r], twin)

    load_l.wait()
    l_z = {d: send(l_row.at[:, own_l], l_row.at[:, own_l], along_z(d)) for d in ORDER}

    load_d.wait()
    d_swap.wait_recv()
    g_row[:, own_g] = (
        (d_own[...].astype(jnp.float32) + d_in[...].astype(jnp.float32)) * 0.5
    ).astype(jnp.bfloat16)

    g_z = {d: send(g_row.at[:, own_g], g_row.at[:, own_g], along_z(d)) for d in ORDER}
    g_x = {d: send(g_row.at[:, own_g], g_row.at[:, own_g], along_x(d)) for d in ORDER}
    slot = len(copies)
    turn = [
        send(g_row.at[pl.ds(HALF * i, HALF), own_g], l_band.at[:, own_g], turned[i], slot + z % 2)
        for i in range(2)
    ]

    def y_sends(refs):
        to_y = {d: [send(r, r, along_y(d)) for r in refs] for d in ORDER}
        return to_y, [send(r, r, mate) for r in refs]

    def y_forwards(to_y, refs_of):
        out = []
        for d in ORDER:
            for cp in to_y[d]:
                cp.wait_recv()
            out += [send(r, r, mate) for r in refs_of((y + 4 - d) % 4)]
        return out

    def r_refs(yy):
        return [r_col.at[rows_at(2 * yy + h, FULL)]]

    def b_refs(yy):
        return [l_band.at[:, lanes(4 * (2 * (1 - h) + i) + yy)] for i in range(2)]

    def m_refs(yy):
        return [m_col.at[rows_at(2 * yy + h, FULL)]]

    load_r.wait()
    r_swap.wait_recv()
    r_y, r_mate = y_sends(r_refs(y))

    rows_a, rows_b = pl.ds(0, SPLIT), pl.ds(SPLIT, FULL - SPLIT)

    def forward_a(buf, chunk):
        ref = buf.at[rows_a, lanes(chunk)]
        return [send(ref, ref, along_x(d)) for d in ORDER]

    def forward_b(buf, chunk):
        ref = buf.at[rows_b, lanes(chunk)]
        return [send(ref, ref, along_z(d)) for d in ORDER]

    g_last = []
    for n, d in enumerate(ORDER):
        g_z[d].wait_recv()
        g_last += forward_a(g_row, 4 * ((z + 4 - d) % 4) + x)
        g_x[d].wait_recv()
        g_last += forward_b(g_row, 4 * z + (x + 4 - d) % 4)
        if n == 0:
            for i in range(2):
                pltpu.make_async_copy(l_band.at[:, own_g], l_band.at[:, own_g], recv_sem.at[slot + i]).wait()
            b_y, b_mate = y_sends(b_refs(y))
    r_mate += y_forwards(r_y, r_refs)
    l_x = {d: send(l_row.at[:, own_l], l_row.at[:, own_l], along_x(d)) for d in ORDER}
    b_mate += y_forwards(b_y, b_refs)
    for cp in g_last:
        cp.wait_recv()
    l_last = []
    for d in ORDER:
        l_z[d].wait_recv()
        l_last += forward_a(l_row, 4 * x + (z + 4 - d) % 4)

    for cp in r_mate:
        cp.wait_recv()
    base = (2 * y + h) * FULL

    @pl.loop(0, 2)
    def _(i):
        tile = nn(g_row[pl.ds(pl.multiple_of(i * HALF, HALF), HALF), :], r_col[...])
        m_col[pl.ds(pl.multiple_of(base + i * HALF, HALF), HALF), :] = tile.astype(jnp.bfloat16)

    m_y, m_mate = y_sends(m_refs(y))

    for d in ORDER:
        l_x[d].wait_recv()
        l_last += forward_b(l_row, 4 * ((x + 4 - d) % 4) + z)

    band = [lanes(4 * z + xl), lanes(4 * z + 2 + xl)]

    @pl.loop(0, 4)
    def _(yy):
        other = g_row[:, lanes(4 * yy + 2 * (1 - h) + rep)]
        for i in range(2):
            q_out[yy, :, pl.ds(HALF * i, HALF)] = tn(other, g_row[:, band[i]]).astype(jnp.bfloat16)

    q_swap = send(q_out, q_in, mate)

    @pl.loop(0, 4)
    def _(yy):
        mine = g_row[:, lanes(4 * yy + 2 * h + rep)]
        for i in range(2):
            q_own[yy, :, pl.ds(HALF * i, HALF)] = tn(mine, g_row[:, band[i]])

    q_swap.wait_recv()

    @pl.loop(0, 4)
    def _(yy):
        total = q_own[yy] + q_in[yy].astype(jnp.float32)
        q_own[yy] = total
        s_out[yy] = total.astype(jnp.bfloat16)

    s_y = [send(s_out.at[(y + d) % 4], s_in.at[n], along_y(d)) for n, d in enumerate(ORDER)]

    for cp in b_mate:
        cp.wait_recv()

    @pl.loop(0, 2)
    def _(i):
        part = pl.ds(pl.multiple_of(i * HALF, HALF), HALF)
        out_left[part, :] = nt(g_row[part, :], l_band[...])

    m_mate += y_forwards(m_y, m_refs)

    for cp in l_last:
        cp.wait_recv()
    for cp in m_mate:
        cp.wait_recv()

    @pl.loop(0, 2)
    def _(i):
        part = pl.ds(pl.multiple_of(i * HALF, HALF), HALF)
        tile = nn(l_row[part, :], m_col[...])
        out_pre[part, lanes(rep)] = tile
        p_out[part, :] = tile.astype(jnp.bfloat16)

    p_swap = send(p_out, p_in, twin)

    for cp in s_y:
        cp.wait_recv()
    out_right[...] = (
        q_own[y] + s_in[0].astype(jnp.float32) + s_in[1].astype(jnp.float32) + s_in[2].astype(jnp.float32)
    )

    p_swap.wait_recv()
    out_pre[:, lanes(1 - rep)] = p_in[...].astype(jnp.float32)

    for cp in copies:
        cp.wait_send()
    assert len(copies) == N_COPIES, len(copies)


def shards(replica_deltas, weights, momentum, left_state, right_state, left_root, right_root):
    total = left_root.shape[0] * lax.axis_size("row")
    bf16, f32 = jnp.bfloat16, jnp.float32
    any_spec = pl.BlockSpec(memory_space=pl.ANY)
    vmem_spec = pl.BlockSpec(memory_space=pltpu.VMEM)
    update, left_gram, right_gram = pl.pallas_call(
        kernel,
        name="shampoo",
        out_shape=(
            jax.ShapeDtypeStruct((FULL, FULL), f32),
            jax.ShapeDtypeStruct((FULL, HALF), f32),
            jax.ShapeDtypeStruct((HALF, FULL), f32),
        ),
        in_specs=[any_spec] * 3,
        out_specs=[vmem_spec] * 3,
        scratch_shapes=[
            pltpu.VMEM((FULL, HALF), bf16),
            pltpu.VMEM((FULL, HALF), bf16),
            pltpu.VMEM((FULL, total), bf16),
            pltpu.VMEM((FULL, total), bf16),
            pltpu.VMEM((total, HALF), bf16),
            pltpu.VMEM((total, HALF), bf16),
            pltpu.VMEM((HALF, total), bf16),
            pltpu.VMEM((4, HALF, FULL), bf16),
            pltpu.VMEM((4, HALF, FULL), f32),
            pltpu.VMEM((4, HALF, FULL), bf16),
            pltpu.VMEM((4, HALF, FULL), bf16),
            pltpu.VMEM((3, HALF, FULL), bf16),
            pltpu.VMEM((FULL, HALF), bf16),
            pltpu.VMEM((FULL, HALF), bf16),
            pltpu.SemaphoreType.DMA((3,)),
            pltpu.SemaphoreType.DMA((N_COPIES,)),
            pltpu.SemaphoreType.DMA((N_COPIES,)),
        ],
        compiler_params=pltpu.CompilerParams(
            collective_id=0, has_side_effects=True, vmem_limit_bytes=56 * 2**20
        ),
        cost_estimate=pl.CostEstimate(flops=8 * 2**30, bytes_accessed=4 * 2**20, transcendentals=0),
    )(replica_deltas[0], left_root, right_root)
    new_left = decay_rate * left_state + (1.0 - decay_rate) / total * left_gram
    new_right = decay_rate * right_state + (1.0 - decay_rate) / total * right_gram
    new_momentum = momentum_rate * momentum + update
    new_weights = weights - outer_rate * (momentum_rate * new_momentum + update)
    return (new_weights, new_momentum, new_left, new_right)


def solution(mesh):
    in_specs = (
        P("rep", "row", "col"),
        P("row", "col"),
        P("row", "col"),
        P("row", ("rep", "col")),
        P(("rep", "row"), "col"),
        P("row", ("rep", "col")),
        P(("rep", "row"), "col"),
    )
    out_specs = (
        P("row", "col"),
        P("row", "col"),
        P("row", ("rep", "col")),
        P(("rep", "row"), "col"),
    )
    return jax.shard_map(shards, mesh=mesh, in_specs=in_specs, out_specs=out_specs, check_vma=False)
```

time: 461 us -> 110 us (0.24)
  waiting for transfers between devices: 411 us -> 0 us
  Pallas kernels: 0 us -> 102 us
  matrix products: 22.8 us -> 0 us
  between operations: 14.2 us -> 0.69 us
  local copies, waits for them, and re-layouts: 7.25 us -> 0.02 us
    all_gather x5 -> x0, waiting for transfers between devices: 215 us -> none  [the longest x1 57.1 us: shards(): left_band = lax.all_gather(left_root, ('rep', 'col'), axis=1, tiled=True)]
    reduce_scatter x2 -> x0, waiting for transfers between devices: 151 us -> none  [the longest x1 81.6 us: shards(): lax.psum_scatter(lax.dot_general(block, mine_rows, contract_first, prefer...]
    pallas_call x0 -> x1, Pallas kernels: none -> 102 us  [shards(): pl.pallas_call(kernel, name='shampoo', out_shape=(jax.ShapeDtypeStruct((F...]
    psum x1 -> x0, waiting for transfers between devices: 41.7 us -> none  [shards(): lax.psum(replica_deltas[0].astype(jnp.float32).astype(jnp.bfloat16), 'rep')]
    dot_general x4 -> x0, matrix products: 22.8 us -> none  [the longest x1 6.6 us: shards(): jnp.dot(block, lax.all_gather(right_root, ('rep', 'row'), axis=0, tiled=T...]
    unnamed x18 -> x10, local copies, waits for them, and re-layouts: 6.45 us -> 0.02 us
  transfers between devices with their start and end apart: 8 -> 0, of which waited for: 8 -> 0; matrix products, arithmetic and copies ran while one was open for 5% -> 0% of each run, Pallas kernels for 0% -> 0%
where the time goes in v1:
time: 110 us; the launch traced here: 109 us
  Pallas kernels  102 us (93%)
  other arithmetic  5.79 us (5%)
    pallas_call x1, Pallas kernels, shards(): pl.pallas_call(kernel, name='shampoo', out_shape=(jax.ShapeDtypeStruct((F...  102 us

profile of v1, /device:TPU:0, one launch (start us, length us, event | category | flops | bytes accessed | tf_op | source)
XLA Modules:
  0.0 108.7 jit_solution(18037922745454144360)
XLA Ops:
  0.6 0.0 copy-start.3
  0.6 0.0 copy-start.4
  0.7 102.2 %shampoo.1 = (f32[512,512]{1,0:T(8,128)}, f32[512,256]{1,0:T(8,128)}, f32[256,512]{1,0:T(8,128)}) custom-call(bf16[512,512]{1,0:T(8,128)(2,1)} %bitcast.1, bf16[512,256]{1,0:T(8,128)(2,1)} %left_root.1, bf16[256,512]{1,0:T(8,128)(2,1)} %right_root.1), custom_call_target="tpu_custom_call" | custom-call | flops 8589934592 | bytes 4194304 | tf_op jit(solution)/shard_map/shampoo/pallas_call | solution.py:260
  102.9 0.0 copy-done.3
  102.9 0.0 copy-start.1
  102.9 0.0 copy-start.2
  102.9 2.1 %multiply_add_fusion.2 = f32[512,256]{1,0:T(8,128)} fusion(f32[512,256]{1,0:T(8,128)} %get-tuple-element.8, f32[512,256]{1,0:T(8,128)S(1)} %copy-done.3), kind=kLoop, calls=%fused_computation.3 | loop fusion | flops 393216 | bytes 1572864 | tf_op jit(solution)/shard_map/add | solution.py:294
  105.0 0.0 copy-done.4
  105.0 0.0 copy-start
  105.0 2.0 %multiply_add_fusion.1 = f32[256,512]{1,0:T(8,128)} fusion(f32[256,512]{1,0:T(8,128)} %get-tuple-element.9, f32[256,512]{1,0:T(8,128)S(1)} %copy-done.4), kind=kLoop, calls=%fused_computation.2 | loop fusion | flops 393216 | bytes 1572864 | tf_op jit(solution)/shard_map/add | solution.py:295
  107.0 0.0 copy-done.1
  107.0 0.0 copy-done.2
  107.0 0.0 copy-done
  107.0 1.7 %multiply_subtract_fusion = (f32[512,512]{1,0:T(8,128)}, f32[512,512]{1,0:T(8,128)}) fusion(f32[512,512]{1,0:T(8,128)S(1)} %copy-done, f32[512,512]{1,0:T(8,128)S(1)} %copy-done.2, f32[512,512]{1,0:T(8,128)S(1)} %copy-done.1), kind=kLoop, calls=%fused_computation | loop fusion | flops 1572864 | bytes 5242880 | tf_op jit(solution)/shard_map/sub | solution.py:297
Async XLA Ops:
  0.6 102.2 %copy-start.3 = (f32[512,256]{1,0:T(8,128)S(1)}, f32[512,256]{1,0:T(8,128)}, u32[]{:S(2)}) copy-start(f32[512,256]{1,0:T(8,128)} %param.10) | copy-start | bytes 1572868
  0.6 104.3 %copy-start.4 = (f32[256,512]{1,0:T(8,128)S(1)}, f32[256,512]{1,0:T(8,128)}, u32[]{:S(2)}) copy-start(f32[256,512]{1,0:T(8,128)} %param.11) | copy-start | bytes 1572868
  102.9 4.1 %copy-start.1 = (f32[512,512]{1,0:T(8,128)S(1)}, f32[512,512]{1,0:T(8,128)}, u32[]{:S(2)}) copy-start(f32[512,512]{1,0:T(8,128)} %param.9) | copy-start | bytes 3145732
  102.9 4.1 %copy-start.2 = (f32[512,512]{1,0:T(8,128)S(1)}, f32[512,512]{1,0:T(8,128)}, u32[]{:S(2)}) copy-start(f32[512,512]{1,0:T(8,128)} %get-tuple-element.7) | copy-start | bytes 3145732
  105.0 2.0 %copy-start = (f32[512,512]{1,0:T(8,128)S(1)}, f32[512,512]{1,0:T(8,128)}, u32[]{:S(2)}) copy-start(f32[512,512]{1,0:T(8,128)} %param.8) | copy-start | bytes 3145732

commit v2 on v1

--- a/solution.py
+++ b/solution.py
@@ -12,11 +12,10 @@
 outer_rate = 0.7
 
 MESH = pl.DeviceIdType.MESH
-ORDER = (1, 3, 2)
 HALF = 256
 FULL = 512
-SPLIT = 256
-N_COPIES = 85
+SPLIT = 160
+N_COPIES = 105
 
 
 def lanes(chunk):
@@ -56,13 +55,13 @@
         return (xx // 2, yy * 2 + hh, (xx % 2) * 4 + zz)
 
     def along_x(d):
-        return dev((x + d) % 4, y, z, h)
+        return dev((x + 4 + d) % 4, y, z, h)
 
     def along_y(d):
-        return dev(x, (y + d) % 4, z, h)
+        return dev(x, (y + 4 + d) % 4, z, h)
 
     def along_z(d):
-        return dev(x, y, (z + d) % 4, h)
+        return dev(x, y, (z + 4 + d) % 4, h)
 
     mate = dev(x, y, z, 1 - h)
     twin = along_x(2)
@@ -82,6 +81,90 @@
         copies.append(cp)
         return cp
 
+    class Ring:
+        def __init__(self, along, at, refs, sign=1, share=False):
+            self.along, self.at, self.refs, self.sign, self.share = along, at, refs, sign, share
+            self.shared = []
+            self.first = {d: self.push(at, None, d) for d in (1, -1)}
+            self.second = {}
+            self.give(at, None)
+
+        def push(self, i, part, d):
+            return [send(r, r, self.along(d)) for r in self.refs(i, part)]
+
+        def give(self, i, part):
+            if self.share:
+                self.shared += [send(r, r, mate) for r in self.refs(i, part)]
+
+        def turn(self, d):
+            for cp in self.first[d]:
+                cp.wait_recv()
+            i = (self.at + 4 - d) % 4
+            self.second[d] = self.push(i, 0 if d == self.sign else 1, d)
+            self.give(i, None)
+
+        def end(self, d):
+            for cp in self.second[d]:
+                cp.wait_recv()
+            self.give((self.at + 2) % 4, 0 if d == self.sign else 1)
+
+        def got(self):
+            for cp in self.shared:
+                cp.wait_recv()
+
+    class Plane:
+        def __init__(self, buf, spot, sign):
+            self.buf, self.spot, self.sign = buf, spot, sign
+            self.rings = []
+
+        def rows(self, lo, hi, xx, zz):
+            return [self.buf.at[pl.ds(lo, hi - lo), lanes(self.spot(xx, zz))]]
+
+        def start_z(self):
+            cuts = {None: (0, FULL), 0: (0, SPLIT), 1: (SPLIT, FULL)}
+            self.z = Ring(along_z, z, lambda i, part: self.rows(*cuts[part], x, i), self.sign)
+
+        def start_x(self):
+            cuts = {None: (0, FULL), 0: (SPLIT, FULL), 1: (0, SPLIT)}
+            self.x = Ring(along_x, x, lambda i, part: self.rows(*cuts[part], i, z), self.sign)
+
+        def on_x(self, zz):
+            cuts = {None: (0, SPLIT), 0: (0, SPLIT // 2), 1: (SPLIT // 2, SPLIT)}
+            self.rings.append(Ring(along_x, x, lambda i, part: self.rows(*cuts[part], i, zz), self.sign))
+
+        def on_z(self, xx):
+            mid = (SPLIT + FULL) // 2
+            cuts = {None: (SPLIT, FULL), 0: (SPLIT, mid), 1: (mid, FULL)}
+            self.rings.append(Ring(along_z, z, lambda i, part: self.rows(*cuts[part], xx, i), self.sign))
+
+        def turn_z(self, d):
+            self.z.turn(d)
+            self.on_x((z + 4 - d) % 4)
+
+        def turn_x(self, d):
+            self.x.turn(d)
+            self.on_z((x + 4 - d) % 4)
+
+        def far_z(self):
+            self.z.end(self.sign)
+            self.on_x((z + 2) % 4)
+
+        def far_x(self):
+            self.x.end(self.sign)
+            self.on_z((x + 2) % 4)
+
+        def turn_rings(self):
+            for ring in self.rings:
+                ring.turn(1)
+                ring.turn(-1)
+
+        def end(self):
+            self.z.end(-self.sign)
+            self.x.end(-self.sign)
+            for ring in self.rings:
+                ring.end(1)
+                ring.end(-1)
+
     own_g = lanes(4 * z + x)
     own_l = lanes(4 * x + z)
     own_r = rows_at(4 * y + 2 * h + rep, HALF)
@@ -93,16 +176,16 @@
     load_r.start()
 
     barrier = pltpu.get_barrier_semaphore()
-    partners = [f(d) for f in (along_x, along_y, along_z) for d in ORDER] + [mate] + turned + turned_from
+    partners = [f(d) for f in (along_x, along_y, along_z) for d in (1, -1)]
+    partners += [twin, mate, along_y(2)] + turned + turned_from
     for partner in partners:
         pl.semaphore_signal(barrier, inc=1, device_id=partner, device_id_type=MESH)
     pl.semaphore_wait(barrier, len(partners))
 
     d_swap = send(delta.at[:, lanes(1 - rep)], d_in, twin)
-    r_swap = send(right_root.at[:, lanes(1 - rep)], r_col.at[own_r], twin)
-
     load_l.wait()
-    l_z = {d: send(l_row.at[:, own_l], l_row.at[:, own_l], along_z(d)) for d in ORDER}
+    left = Plane(l_row, lambda xx, zz: 4 * xx + zz, -1)
+    left.start_z()
 
     load_d.wait()
     d_swap.wait_recv()
@@ -110,71 +193,59 @@
         (d_own[...].astype(jnp.float32) + d_in[...].astype(jnp.float32)) * 0.5
     ).astype(jnp.bfloat16)
 
-    g_z = {d: send(g_row.at[:, own_g], g_row.at[:, own_g], along_z(d)) for d in ORDER}
-    g_x = {d: send(g_row.at[:, own_g], g_row.at[:, own_g], along_x(d)) for d in ORDER}
+    grad = Plane(g_row, lambda xx, zz: 4 * zz + xx, 1)
+    grad.start_x()
+    grad.start_z()
     slot = len(copies)
     turn = [
         send(g_row.at[pl.ds(HALF * i, HALF), own_g], l_band.at[:, own_g], turned[i], slot + z % 2)
         for i in range(2)
     ]
-
-    def y_sends(refs):
-        to_y = {d: [send(r, r, along_y(d)) for r in refs] for d in ORDER}
-        return to_y, [send(r, r, mate) for r in refs]
-
-    def y_forwards(to_y, refs_of):
-        out = []
-        for d in ORDER:
-            for cp in to_y[d]:
-                cp.wait_recv()
-            out += [send(r, r, mate) for r in refs_of((y + 4 - d) % 4)]
-        return out
-
-    def r_refs(yy):
-        return [r_col.at[rows_at(2 * yy + h, FULL)]]
-
-    def b_refs(yy):
-        return [l_band.at[:, lanes(4 * (2 * (1 - h) + i) + yy)] for i in range(2)]
-
-    def m_refs(yy):
-        return [m_col.at[rows_at(2 * yy + h, FULL)]]
-
+    r_swap = send(right_root.at[:, lanes(1 - rep)], r_col.at[own_r], twin)
+    left.z.turn(1)
+    left.z.turn(-1)
+
+    def pair(buf):
+        def refs(yy, part):
+            base, size = (2 * yy + h) * FULL, FULL
+            if part is not None:
+                base, size = base + part * HALF, HALF
+            return [buf.at[pl.ds(pl.multiple_of(base, HALF), size)]]
+
+        return refs
+
+    def band_refs(yy, part):
+        return [
+            l_band.at[:, lanes(4 * (2 * (1 - h) + i) + yy)]
+            for i in ((0, 1) if part is None else (part,))
+        ]
+
+    grad.turn_x(1)
+    grad.turn_z(1)
+    grad.turn_x(-1)
+    grad.turn_z(-1)
     load_r.wait()
     r_swap.wait_recv()
-    r_y, r_mate = y_sends(r_refs(y))
-
-    rows_a, rows_b = pl.ds(0, SPLIT), pl.ds(SPLIT, FULL - SPLIT)
-
-    def forward_a(buf, chunk):
-        ref = buf.at[rows_a, lanes(chunk)]
-        return [send(ref, ref, along_x(d)) for d in ORDER]
-
-    def forward_b(buf, chunk):
-        ref = buf.at[rows_b, lanes(chunk)]
-        return [send(ref, ref, along_z(d)) for d in ORDER]
-
-    g_last = []
-    for n, d in enumerate(ORDER):
-        g_z[d].wait_recv()
-        g_last += forward_a(g_row, 4 * ((z + 4 - d) % 4) + x)
-        g_x[d].wait_recv()
-        g_last += forward_b(g_row, 4 * z + (x + 4 - d) % 4)
-        if n == 0:
-            for i in range(2):
-                pltpu.make_async_copy(l_band.at[:, own_g], l_band.at[:, own_g], recv_sem.at[slot + i]).wait()
-            b_y, b_mate = y_sends(b_refs(y))
-    r_mate += y_forwards(r_y, r_refs)
-    l_x = {d: send(l_row.at[:, own_l], l_row.at[:, own_l], along_x(d)) for d in ORDER}
-    b_mate += y_forwards(b_y, b_refs)
-    for cp in g_last:
-        cp.wait_recv()
-    l_last = []
-    for d in ORDER:
-        l_z[d].wait_recv()
-        l_last += forward_a(l_row, 4 * x + (z + 4 - d) % 4)
-
-    for cp in r_mate:
-        cp.wait_recv()
+    r_ring = Ring(along_y, y, pair(r_col), share=True)
+    grad.far_x()
+    grad.far_z()
+    for i in range(2):
+        pltpu.make_async_copy(l_band.at[:, own_g], l_band.at[:, own_g], recv_sem.at[slot + i]).wait()
+    b_ring = Ring(along_y, y, band_refs, share=True)
+    grad.turn_rings()
+    left.start_x()
+    for ring in (r_ring, b_ring):
+        ring.turn(1)
+        ring.turn(-1)
+    grad.end()
+    left.on_x((z + 3) % 4)
+    left.on_x((z + 1) % 4)
+    left.far_z()
+    for ring in (r_ring, b_ring):
+        ring.end(1)
+        ring.end(-1)
+    r_ring.got()
+
     base = (2 * y + h) * FULL
 
     @pl.loop(0, 2)
@@ -182,11 +253,10 @@
         tile = nn(g_row[pl.ds(pl.multiple_of(i * HALF, HALF), HALF), :], r_col[...])
         m_col[pl.ds(pl.multiple_of(base + i * HALF, HALF), HALF), :] = tile.astype(jnp.bfloat16)
 
-    m_y, m_mate = y_sends(m_refs(y))
-
-    for d in ORDER:
-        l_x[d].wait_recv()
-        l_last += forward_b(l_row, 4 * ((x + 4 - d) % 4) + z)
+    m_ring = Ring(along_y, y, pair(m_col), share=True)
+
+    left.turn_x(1)
+    left.turn_x(-1)
 
     band = [lanes(4 * z + xl), lanes(4 * z + 2 + xl)]
 
@@ -197,6 +267,10 @@
             q_out[yy, :, pl.ds(HALF * i, HALF)] = tn(other, g_row[:, band[i]]).astype(jnp.bfloat16)
 
     q_swap = send(q_out, q_in, mate)
+    left.far_x()
+    left.turn_rings()
+    m_ring.turn(1)
+    m_ring.turn(-1)
 
     @pl.loop(0, 4)
     def _(yy):
@@ -212,22 +286,19 @@
         q_own[yy] = total
         s_out[yy] = total.astype(jnp.bfloat16)
 
-    s_y = [send(s_out.at[(y + d) % 4], s_in.at[n], along_y(d)) for n, d in enumerate(ORDER)]
-
-    for cp in b_mate:
-        cp.wait_recv()
+    s_y = [send(s_out.at[(y + 4 + d) % 4], s_in.at[n], along_y(d)) for n, d in enumerate((1, -1, 2))]
+    m_ring.end(1)
+    m_ring.end(-1)
+
+    b_ring.got()
 
     @pl.loop(0, 2)
     def _(i):
         part = pl.ds(pl.multiple_of(i * HALF, HALF), HALF)
         out_left[part, :] = nt(g_row[part, :], l_band[...])
 
-    m_mate += y_forwards(m_y, m_refs)
-
-    for cp in l_last:
-        cp.wait_recv()
-    for cp in m_mate:
-        cp.wait_recv()
+    left.end()
+    m_ring.got()
 
     @pl.loop(0, 2)
     def _(i):

time: 110 us -> 99.2 us (0.902)
  the two profiles are of different devices: /device:TPU:0 before, /device:TPU:34 now
where the time goes in v2:
time: 99.2 us; the launch traced here: 99.1 us
  Pallas kernels  92.6 us (93%)
  other arithmetic  5.79 us (6%)
    pallas_call x1, Pallas kernels, shards(): pl.pallas_call(kernel, name='shampoo', out_shape=(jax.ShapeDtypeStruct((F...  92.6 us
    add x1, other arithmetic, shards(): new_left = decay_rate * left_state + (1.0 - decay_rate) / total * left_gram  2.07 us
    add x1, other arithmetic, shards(): decay_rate * right_state + (1.0 - decay_rate) / total * right_gram  2.03 us

profile of v2, /device:TPU:34, one launch (start us, length us, event | category | flops | bytes accessed | tf_op | source)
XLA Modules:
  0.0 99.1 jit_solution(12575978277749071229)
XLA Ops:
  0.6 0.0 copy-start.3
  0.6 0.0 copy-start.4
  0.7 92.6 %shampoo.1 = (f32[512,512]{1,0:T(8,128)}, f32[512,256]{1,0:T(8,128)}, f32[256,512]{1,0:T(8,128)}) custom-call(bf16[512,512]{1,0:T(8,128)(2,1)} %bitcast.1, bf16[512,256]{1,0:T(8,128)(2,1)} %left_root.1, bf16[256,512]{1,0:T(8,128)(2,1)} %right_root.1), custom_call_target="tpu_custom_call" | custom-call | flops 8589934592 | bytes 4194304 | tf_op jit(solution)/shard_map/shampoo/pallas_call | solution.py:331
  93.2 0.0 copy-done.3
  93.2 0.0 copy-start.1
  93.2 0.0 copy-start.2
  93.3 2.1 %multiply_add_fusion.2 = f32[512,256]{1,0:T(8,128)} fusion(f32[512,256]{1,0:T(8,128)} %get-tuple-element.8, f32[512,256]{1,0:T(8,128)S(1)} %copy-done.3), kind=kLoop, calls=%fused_computation.3 | loop fusion | flops 393216 | bytes 1572864 | tf_op jit(solution)/shard_map/add | solution.py:365
  95.3 0.0 copy-done.4
  95.3 0.0 copy-start
  95.3 2.0 %multiply_add_fusion.1 = f32[256,512]{1,0:T(8,128)} fusion(f32[256,512]{1,0:T(8,128)} %get-tuple-element.9, f32[256,512]{1,0:T(8,128)S(1)} %copy-done.4), kind=kLoop, calls=%fused_computation.2 | loop fusion | flops 393216 | bytes 1572864 | tf_op jit(solution)/shard_map/add | solution.py:366
  97.4 0.0 copy-done.1
  97.4 0.0 copy-done.2
  97.4 0.0 copy-done
  97.4 1.7 %multiply_subtract_fusion = (f32[512,512]{1,0:T(8,128)}, f32[512,512]{1,0:T(8,128)}) fusion(f32[512,512]{1,0:T(8,128)S(1)} %copy-done, f32[512,512]{1,0:T(8,128)S(1)} %copy-done.2, f32[512,512]{1,0:T(8,128)S(1)} %copy-done.1), kind=kLoop, calls=%fused_computation | loop fusion | flops 1572864 | bytes 5242880 | tf_op jit(solution)/shard_map/sub | solution.py:368
Async XLA Ops:
  0.6 92.6 %copy-start.3 = (f32[512,256]{1,0:T(8,128)S(1)}, f32[512,256]{1,0:T(8,128)}, u32[]{:S(2)}) copy-start(f32[512,256]{1,0:T(8,128)} %param.10) | copy-start | bytes 1572868
  0.6 94.7 %copy-start.4 = (f32[256,512]{1,0:T(8,128)S(1)}, f32[256,512]{1,0:T(8,128)}, u32[]{:S(2)}) copy-start(f32[256,512]{1,0:T(8,128)} %param.11) | copy-start | bytes 1572868
  93.2 4.1 %copy-start.1 = (f32[512,512]{1,0:T(8,128)S(1)}, f32[512,512]{1,0:T(8,128)}, u32[]{:S(2)}) copy-start(f32[512,512]{1,0:T(8,128)} %param.9) | copy-start | bytes 3145732
  93.2 4.1 %copy-start.2 = (f32[512,512]{1,0:T(8,128)S(1)}, f32[512,512]{1,0:T(8,128)}, u32[]{:S(2)}) copy-start(f32[512,512]{1,0:T(8,128)} %get-tuple-element.7) | copy-start | bytes 3145732
  95.3 2.0 %copy-start = (f32[512,512]{1,0:T(8,128)S(1)}, f32[512,512]{1,0:T(8,128)}, u32[]{:S(2)}) copy-start(f32[512,512]{1,0:T(8,128)} %param.8) | copy-start | bytes 3145732

commit v3 on v2

--- a/solution.py
+++ b/solution.py
@@ -14,8 +14,9 @@
 MESH = pl.DeviceIdType.MESH
 HALF = 256
 FULL = 512
-SPLIT = 160
-N_COPIES = 105
+QUARTER = 64
+SPLIT = 224
+N_COPIES = 131
 
 
 def lanes(chunk):
@@ -42,7 +43,7 @@
     delta, left_root, right_root,
     out_pre, out_left, out_right,
     d_own, d_in, g_row, l_row, r_col, m_col, l_band,
-    q_out, q_own, q_in, s_out, s_in, p_out, p_in,
+    b_part, q_out, q_own, q_in, s_out, s_in, p_out, p_in,
     local_sem, send_sem, recv_sem,
 ):
     rep = lax.axis_index("rep")
@@ -65,8 +66,8 @@
 
     mate = dev(x, y, z, 1 - h)
     twin = along_x(2)
-    turned = [dev(y, x, 2 * h + i, 1 - z // 2) for i in range(2)]
-    turned_from = [dev(y, x, 2 * (1 - h) + i, z // 2) for i in range(2)]
+    turned = [[dev((y + 4 - d) % 4, y, 2 * h + i, 1 - z // 2) for i in range(2)] for d in range(4)]
+    turned_from = [dev(xx, y, 2 * (1 - h) + i, z // 2) for xx in range(4) for i in range(2)]
 
     copies = []
 
@@ -82,8 +83,8 @@
         return cp
 
     class Ring:
-        def __init__(self, along, at, refs, sign=1, share=False):
-            self.along, self.at, self.refs, self.sign, self.share = along, at, refs, sign, share
+        def __init__(self, along, at, refs, onward, share=False):
+            self.along, self.at, self.refs, self.onward, self.share = along, at, refs, onward, share
             self.shared = []
             self.first = {d: self.push(at, None, d) for d in (1, -1)}
             self.second = {}
@@ -100,57 +101,71 @@
             for cp in self.first[d]:
                 cp.wait_recv()
             i = (self.at + 4 - d) % 4
-            self.second[d] = self.push(i, 0 if d == self.sign else 1, d)
+            if d in self.onward:
+                self.second[d] = self.push(i, self.onward[d], d)
             self.give(i, None)
 
         def end(self, d):
             for cp in self.second[d]:
                 cp.wait_recv()
-            self.give((self.at + 2) % 4, 0 if d == self.sign else 1)
+            self.give((self.at + 2) % 4, self.onward[d])
 
         def got(self):
             for cp in self.shared:
                 cp.wait_recv()
 
+    halves = {1: 0, -1: 1}
+    spans = ((0, SPLIT), (SPLIT, FULL))
+
     class Plane:
         def __init__(self, buf, spot, sign):
             self.buf, self.spot, self.sign = buf, spot, sign
-            self.rings = []
-
-        def rows(self, lo, hi, xx, zz):
+            self.rings, self.z, self.x = [], [None, None], [None, None]
+
+        def rows(self, span, part, xx, zz):
+            lo, hi = span
+            mid = (lo + hi) // 2
+            lo, hi = {None: (lo, hi), 0: (lo, mid), 1: (mid, hi)}[part]
             return [self.buf.at[pl.ds(lo, hi - lo), lanes(self.spot(xx, zz))]]
 
-        def start_z(self):
-            cuts = {None: (0, FULL), 0: (0, SPLIT), 1: (SPLIT, FULL)}
-            self.z = Ring(along_z, z, lambda i, part: self.rows(*cuts[part], x, i), self.sign)
-
-        def start_x(self):
-            cuts = {None: (0, FULL), 0: (SPLIT, FULL), 1: (0, SPLIT)}
-            self.x = Ring(along_x, x, lambda i, part: self.rows(*cuts[part], i, z), self.sign)
+        def start_z(self, k):
+            refs = lambda i, part: self.rows(spans[k], part, x, i)
+            self.z[k] = Ring(along_z, z, refs, {self.sign if k == 0 else -self.sign: None})
+
+        def start_x(self, k):
+            refs = lambda i, part: self.rows(spans[k], part, i, z)
+            self.x[k] = Ring(along_x, x, refs, {self.sign if k == 1 else -self.sign: None})
 
         def on_x(self, zz):
-            cuts = {None: (0, SPLIT), 0: (0, SPLIT // 2), 1: (SPLIT // 2, SPLIT)}
-            self.rings.append(Ring(along_x, x, lambda i, part: self.rows(*cuts[part], i, zz), self.sign))
+            refs = lambda i, part: self.rows(spans[0], part, i, zz)
+            self.rings.append(Ring(along_x, x, refs, halves))
 
         def on_z(self, xx):
-            mid = (SPLIT + FULL) // 2
-            cuts = {None: (SPLIT, FULL), 0: (SPLIT, mid), 1: (mid, FULL)}
-            self.rings.append(Ring(along_z, z, lambda i, part: self.rows(*cuts[part], xx, i), self.sign))
-
-        def turn_z(self, d):
-            self.z.turn(d)
-            self.on_x((z + 4 - d) % 4)
-
-        def turn_x(self, d):
-            self.x.turn(d)
-            self.on_z((x + 4 - d) % 4)
+            refs = lambda i, part: self.rows(spans[1], part, xx, i)
+            self.rings.append(Ring(along_z, z, refs, halves))
+
+        def turn_z(self, k):
+            for d in (self.sign, -self.sign):
+                self.z[k].turn(d)
+
+        def turn_x(self, k):
+            for d in (self.sign, -self.sign):
+                self.x[k].turn(d)
+
+        def near_z(self):
+            self.on_x((z + 4 - self.sign) % 4)
+            self.on_x((z + 4 + self.sign) % 4)
+
+        def near_x(self):
+            self.on_z((x + 4 - self.sign) % 4)
+            self.on_z((x + 4 + self.sign) % 4)
 
         def far_z(self):
-            self.z.end(self.sign)
+            self.z[0].end(self.sign)
             self.on_x((z + 2) % 4)
 
         def far_x(self):
-            self.x.end(self.sign)
+            self.x[1].end(self.sign)
             self.on_z((x + 2) % 4)
 
         def turn_rings(self):
@@ -159,8 +174,8 @@
                 ring.turn(-1)
 
         def end(self):
-            self.z.end(-self.sign)
-            self.x.end(-self.sign)
+            self.z[1].end(-self.sign)
+            self.x[0].end(-self.sign)
             for ring in self.rings:
                 ring.end(1)
                 ring.end(-1)
@@ -177,33 +192,43 @@
 
     barrier = pltpu.get_barrier_semaphore()
     partners = [f(d) for f in (along_x, along_y, along_z) for d in (1, -1)]
-    partners += [twin, mate, along_y(2)] + turned + turned_from
+    partners += [twin, mate, along_y(2)] + sum(turned, []) + turned_from
     for partner in partners:
         pl.semaphore_signal(barrier, inc=1, device_id=partner, device_id_type=MESH)
     pl.semaphore_wait(barrier, len(partners))
 
-    d_swap = send(delta.at[:, lanes(1 - rep)], d_in, twin)
+    d_swap = []
+    for lo, hi in spans:
+        part = pl.ds(lo, hi - lo)
+        d_swap.append(send(delta.at[part, lanes(1 - rep)], d_in.at[part, :], twin))
     load_l.wait()
     left = Plane(l_row, lambda xx, zz: 4 * xx + zz, -1)
-    left.start_z()
+    left.start_z(0)
+    left.start_z(1)
 
     load_d.wait()
-    d_swap.wait_recv()
-    g_row[:, own_g] = (
-        (d_own[...].astype(jnp.float32) + d_in[...].astype(jnp.float32)) * 0.5
-    ).astype(jnp.bfloat16)
-
     grad = Plane(g_row, lambda xx, zz: 4 * zz + xx, 1)
-    grad.start_x()
-    grad.start_z()
-    slot = len(copies)
-    turn = [
-        send(g_row.at[pl.ds(HALF * i, HALF), own_g], l_band.at[:, own_g], turned[i], slot + z % 2)
-        for i in range(2)
-    ]
+    for k, (lo, hi) in enumerate(spans):
+        part = pl.ds(lo, hi - lo)
+        d_swap[k].wait_recv()
+        g_row[part, own_g] = (
+            (d_own[part, :].astype(jnp.float32) + d_in[part, :].astype(jnp.float32)) * 0.5
+        ).astype(jnp.bfloat16)
+        grad.start_z(k)
+        grad.start_x(k)
+    spread = {
+        d: [
+            send(
+                g_row.at[pl.ds(pl.multiple_of(HALF * i + QUARTER * ((y + d) % 4), QUARTER), QUARTER), own_g],
+                b_part.at[d - 1, i], along_y(d),
+            )
+            for i in range(2)
+        ]
+        for d in (1, 3, 2)
+    }
     r_swap = send(right_root.at[:, lanes(1 - rep)], r_col.at[own_r], twin)
-    left.z.turn(1)
-    left.z.turn(-1)
+    left.turn_z(0)
+    left.turn_z(1)
 
     def pair(buf):
         def refs(yy, part):
@@ -214,32 +239,49 @@
 
         return refs
 
+    side = pl.ds(pl.multiple_of((1 - h) * 8 * HALF, HALF), 8 * HALF)
+
     def band_refs(yy, part):
-        return [
-            l_band.at[:, lanes(4 * (2 * (1 - h) + i) + yy)]
-            for i in ((0, 1) if part is None else (part,))
-        ]
-
+        lo, size = QUARTER * yy, QUARTER
+        if part is not None:
+            lo, size = lo + part * (QUARTER // 2), QUARTER // 2
+        return [l_band.at[pl.ds(pl.multiple_of(lo, QUARTER // 2), size), side]]
+
+    grad.turn_z(0)
+    grad.near_z()
+    grad.turn_x(0)
+    turn = []
+    slot = len(copies)
+    own_q = pl.ds(pl.multiple_of(QUARTER * y, QUARTER), QUARTER)
+    for d in (0, 1, 3, 2):
+        for i in range(2):
+            if d == 0:
+                src = g_row.at[pl.ds(pl.multiple_of(HALF * i + QUARTER * y, QUARTER), QUARTER), own_g]
+            else:
+                spread[d][i].wait_recv()
+                src = b_part.at[d - 1, i]
+            turn.append(send(src, l_band.at[own_q, own_g], turned[d][i], slot + 2 * x + z % 2))
+    grad.turn_z(1)
     grad.turn_x(1)
-    grad.turn_z(1)
-    grad.turn_x(-1)
-    grad.turn_z(-1)
+    grad.near_x()
     load_r.wait()
     r_swap.wait_recv()
-    r_ring = Ring(along_y, y, pair(r_col), share=True)
+    r_ring = Ring(along_y, y, pair(r_col), halves, share=True)
+    grad.far_z()
     grad.far_x()
-    grad.far_z()
-    for i in range(2):
-        pltpu.make_async_copy(l_band.at[:, own_g], l_band.at[:, own_g], recv_sem.at[slot + i]).wait()
-    b_ring = Ring(along_y, y, band_refs, share=True)
+    for i in range(8):
+        pltpu.make_async_copy(
+            l_band.at[own_q, own_g], l_band.at[own_q, own_g], recv_sem.at[slot + i]
+        ).wait()
+    b_ring = Ring(along_y, y, band_refs, halves, share=True)
     grad.turn_rings()
-    left.start_x()
+    left.start_x(1)
+    left.start_x(0)
     for ring in (r_ring, b_ring):
         ring.turn(1)
         ring.turn(-1)
     grad.end()
-    left.on_x((z + 3) % 4)
-    left.on_x((z + 1) % 4)
+    left.near_z()
     left.far_z()
     for ring in (r_ring, b_ring):
         ring.end(1)
@@ -248,15 +290,24 @@
 
     base = (2 * y + h) * FULL
 
-    @pl.loop(0, 2)
-    def _(i):
-        tile = nn(g_row[pl.ds(pl.multiple_of(i * HALF, HALF), HALF), :], r_col[...])
-        m_col[pl.ds(pl.multiple_of(base + i * HALF, HALF), HALF), :] = tile.astype(jnp.bfloat16)
-
-    m_ring = Ring(along_y, y, pair(m_col), share=True)
+    def m_part(k):
+        def refs(yy, part):
+            lo, size = (2 * yy + h) * FULL + k * HALF, HALF
+            if part is not None:
+                lo, size = lo + part * (HALF // 2), HALF // 2
+            return [m_col.at[pl.ds(pl.multiple_of(lo, HALF // 2), size)]]
+
+        return refs
+
+    m_rings = []
+    for k in range(2):
+        tile = nn(g_row[pl.ds(k * HALF, HALF), :], r_col[...])
+        m_col[pl.ds(pl.multiple_of(base + k * HALF, HALF), HALF), :] = tile.astype(jnp.bfloat16)
+        m_rings.append(Ring(along_y, y, m_part(k), halves, share=True))
 
     left.turn_x(1)
-    left.turn_x(-1)
+    left.near_x()
+    left.turn_x(0)
 
     band = [lanes(4 * z + xl), lanes(4 * z + 2 + xl)]
 
@@ -269,8 +320,9 @@
     q_swap = send(q_out, q_in, mate)
     left.far_x()
     left.turn_rings()
-    m_ring.turn(1)
-    m_ring.turn(-1)
+    for ring in m_rings:
+        ring.turn(1)
+        ring.turn(-1)
 
     @pl.loop(0, 4)
     def _(yy):
@@ -287,8 +339,9 @@
         s_out[yy] = total.astype(jnp.bfloat16)
 
     s_y = [send(s_out.at[(y + 4 + d) % 4], s_in.at[n], along_y(d)) for n, d in enumerate((1, -1, 2))]
-    m_ring.end(1)
-    m_ring.end(-1)
+    for ring in m_rings:
+        ring.end(1)
+        ring.end(-1)
 
     b_ring.got()
 
@@ -298,16 +351,16 @@
         out_left[part, :] = nt(g_row[part, :], l_band[...])
 
     left.end()
-    m_ring.got()
-
-    @pl.loop(0, 2)
-    def _(i):
-        part = pl.ds(pl.multiple_of(i * HALF, HALF), HALF)
+    for ring in m_rings:
+        ring.got()
+
+    p_swap = []
+    for k in range(2):
+        part = pl.ds(k * HALF, HALF)
         tile = nn(l_row[part, :], m_col[...])
+        p_out[part, :] = tile.astype(jnp.bfloat16)
+        p_swap.append(send(p_out.at[part, :], p_in.at[part, :], twin))
         out_pre[part, lanes(rep)] = tile
-        p_out[part, :] = tile.astype(jnp.bfloat16)
-
-    p_swap = send(p_out, p_in, twin)
 
     for cp in s_y:
         cp.wait_recv()
@@ -315,8 +368,10 @@
         q_own[y] + s_in[0].astype(jnp.float32) + s_in[1].astype(jnp.float32) + s_in[2].astype(jnp.float32)
     )
 
-    p_swap.wait_recv()
-    out_pre[:, lanes(1 - rep)] = p_in[...].astype(jnp.float32)
+    for k in range(2):
+        part = pl.ds(k * HALF, HALF)
+        p_swap[k].wait_recv()
+        out_pre[part, lanes(1 - rep)] = p_in[part, :].astype(jnp.float32)
 
     for cp in copies:
         cp.wait_send()
@@ -346,6 +401,7 @@
             pltpu.VMEM((total, HALF), bf16),
             pltpu.VMEM((total, HALF), bf16),
             pltpu.VMEM((HALF, total), bf16),
+            pltpu.VMEM((3, 2, QUARTER, HALF), bf16),
             pltpu.VMEM((4, HALF, FULL), bf16),
             pltpu.VMEM((4, HALF, FULL), f32),
             pltpu.VMEM((4, HALF, FULL), bf16),

time: 99.2 us -> 93.7 us (0.945)
  the two profiles are of different devices: /device:TPU:34 before, /device:TPU:0 now
where the time goes in v3:
time: 93.7 us; the launch traced here: 93.4 us
  Pallas kernels  86.9 us (93%)
  other arithmetic  5.79 us (6%)
    pallas_call x1, Pallas kernels, shards(): pl.pallas_call(kernel, name='shampoo', out_shape=(jax.ShapeDtypeStruct((F...  86.9 us
    add x1, other arithmetic, shards(): new_left = decay_rate * left_state + (1.0 - decay_rate) / total * left_gram  2.07 us
    add x1, other arithmetic, shards(): decay_rate * right_state + (1.0 - decay_rate) / total * right_gram  2.03 us

profile of v3, /device:TPU:0, one launch (start us, length us, event | category | flops | bytes accessed | tf_op | source)
XLA Modules:
  0.0 93.4 jit_solution(6591903841903008571)
XLA Ops:
  0.6 0.0 copy-start.3
  0.6 0.0 copy-start.4
  0.7 86.9 %shampoo.1 = (f32[512,512]{1,0:T(8,128)}, f32[512,256]{1,0:T(8,128)}, f32[256,512]{1,0:T(8,128)}) custom-call(bf16[512,512]{1,0:T(8,128)(2,1)} %bitcast.1, bf16[512,256]{1,0:T(8,128)(2,1)} %left_root.1, bf16[256,512]{1,0:T(8,128)(2,1)} %right_root.1), custom_call_target="tpu_custom_call" | custom-call | flops 8589934592 | bytes 4194304 | tf_op jit(solution)/shard_map/shampoo/pallas_call | solution.py:386
  87.5 0.0 copy-done.3
  87.6 0.0 copy-start.1
  87.6 0.0 copy-start.2
  87.6 2.1 %multiply_add_fusion.2 = f32[512,256]{1,0:T(8,128)} fusion(f32[512,256]{1,0:T(8,128)} %get-tuple-element.8, f32[512,256]{1,0:T(8,128)S(1)} %copy-done.3), kind=kLoop, calls=%fused_computation.3 | loop fusion | flops 393216 | bytes 1572864 | tf_op jit(solution)/shard_map/add | solution.py:421
  89.6 0.0 copy-done.4
  89.6 0.0 copy-start
  89.6 2.0 %multiply_add_fusion.1 = f32[256,512]{1,0:T(8,128)} fusion(f32[256,512]{1,0:T(8,128)} %get-tuple-element.9, f32[256,512]{1,0:T(8,128)S(1)} %copy-done.4), kind=kLoop, calls=%fused_computation.2 | loop fusion | flops 393216 | bytes 1572864 | tf_op jit(solution)/shard_map/add | solution.py:422
  91.7 0.0 copy-done.1
  91.7 0.0 copy-done.2
  91.7 0.0 copy-done
  91.7 1.7 %multiply_subtract_fusion = (f32[512,512]{1,0:T(8,128)}, f32[512,512]{1,0:T(8,128)}) fusion(f32[512,512]{1,0:T(8,128)S(1)} %copy-done, f32[512,512]{1,0:T(8,128)S(1)} %copy-done.2, f32[512,512]{1,0:T(8,128)S(1)} %copy-done.1), kind=kLoop, calls=%fused_computation | loop fusion | flops 1572864 | bytes 5242880 | tf_op jit(solution)/shard_map/sub | solution.py:424
Async XLA Ops:
  0.6 86.9 %copy-start.3 = (f32[512,256]{1,0:T(8,128)S(1)}, f32[512,256]{1,0:T(8,128)}, u32[]{:S(2)}) copy-start(f32[512,256]{1,0:T(8,128)} %param.10) | copy-start | bytes 1572868
  0.6 89.0 %copy-start.4 = (f32[256,512]{1,0:T(8,128)S(1)}, f32[256,512]{1,0:T(8,128)}, u32[]{:S(2)}) copy-start(f32[256,512]{1,0:T(8,128)} %param.11) | copy-start | bytes 1572868
  87.6 4.1 %copy-start.1 = (f32[512,512]{1,0:T(8,128)S(1)}, f32[512,512]{1,0:T(8,128)}, u32[]{:S(2)}) copy-start(f32[512,512]{1,0:T(8,128)} %param.9) | copy-start | bytes 3145732
  87.6 4.1 %copy-start.2 = (f32[512,512]{1,0:T(8,128)S(1)}, f32[512,512]{1,0:T(8,128)}, u32[]{:S(2)}) copy-start(f32[512,512]{1,0:T(8,128)} %get-tuple-element.7) | copy-start | bytes 3145732
  89.6 2.0 %copy-start = (f32[512,512]{1,0:T(8,128)S(1)}, f32[512,512]{1,0:T(8,128)}, u32[]{:S(2)}) copy-start(f32[512,512]{1,0:T(8,128)} %param.8) | copy-start | bytes 3145732

commit v4 on v3

--- a/solution.py
+++ b/solution.py
@@ -40,10 +40,10 @@
 
 
 def kernel(
-    delta, left_root, right_root,
+    delta, left_root, right_root, left_state, right_state,
     out_pre, out_left, out_right,
     d_own, d_in, g_row, l_row, r_col, m_col, l_band,
-    b_part, q_out, q_own, q_in, s_out, s_in, p_out, p_in,
+    b_part, q_out, q_own, q_in, s_out, s_in, p_out, p_in, state_l, state_r,
     local_sem, send_sem, recv_sem,
 ):
     rep = lax.axis_index("rep")
@@ -173,12 +173,12 @@
                 ring.turn(1)
                 ring.turn(-1)
 
-        def end(self):
-            self.z[1].end(-self.sign)
-            self.x[0].end(-self.sign)
+        def end(self, k):
+            (self.x, self.z)[k][k].end(-self.sign)
             for ring in self.rings:
-                ring.end(1)
-                ring.end(-1)
+                if ring.along is (along_x, along_z)[k]:
+                    ring.end(1)
+                    ring.end(-1)
 
     own_g = lanes(4 * z + x)
     own_l = lanes(4 * x + z)
@@ -189,6 +189,8 @@
     load_d.start()
     load_l.start()
     load_r.start()
+    load_sl = pltpu.make_async_copy(left_state, state_l, local_sem.at[3])
+    load_sr = pltpu.make_async_copy(right_state, state_r, local_sem.at[4])
 
     barrier = pltpu.get_barrier_semaphore()
     partners = [f(d) for f in (along_x, along_y, along_z) for d in (1, -1)]
@@ -265,6 +267,8 @@
     grad.turn_x(1)
     grad.near_x()
     load_r.wait()
+    load_sl.start()
+    load_sr.start()
     r_swap.wait_recv()
     r_ring = Ring(along_y, y, pair(r_col), halves, share=True)
     grad.far_z()
@@ -280,7 +284,6 @@
     for ring in (r_ring, b_ring):
         ring.turn(1)
         ring.turn(-1)
-    grad.end()
     left.near_z()
     left.far_z()
     for ring in (r_ring, b_ring):
@@ -292,17 +295,18 @@
 
     def m_part(k):
         def refs(yy, part):
-            lo, size = (2 * yy + h) * FULL + k * HALF, HALF
-            if part is not None:
-                lo, size = lo + part * (HALF // 2), HALF // 2
-            return [m_col.at[pl.ds(pl.multiple_of(lo, HALF // 2), size)]]
+            lo, hi = spans[k]
+            mid = (lo + hi) // 2
+            lo, hi = {None: (lo, hi), 0: (lo, mid), 1: (mid, hi)}[part]
+            return [m_col.at[pl.ds(pl.multiple_of((2 * yy + h) * FULL + lo, 16), hi - lo)]]
 
         return refs
 
     m_rings = []
-    for k in range(2):
-        tile = nn(g_row[pl.ds(k * HALF, HALF), :], r_col[...])
-        m_col[pl.ds(pl.multiple_of(base + k * HALF, HALF), HALF), :] = tile.astype(jnp.bfloat16)
+    for k, (lo, hi) in enumerate(spans):
+        grad.end(k)
+        tile = nn(g_row[pl.ds(lo, hi - lo), :], r_col[...])
+        m_col[pl.ds(pl.multiple_of(base + lo, 16), hi - lo), :] = tile.astype(jnp.bfloat16)
         m_rings.append(Ring(along_y, y, m_part(k), halves, share=True))
 
     left.turn_x(1)
@@ -343,20 +347,22 @@
         ring.end(1)
         ring.end(-1)
 
+    gain = (1.0 - decay_rate) / g_row.shape[1]
+    load_sl.wait()
+    load_sr.wait()
     b_ring.got()
 
     @pl.loop(0, 2)
     def _(i):
         part = pl.ds(pl.multiple_of(i * HALF, HALF), HALF)
-        out_left[part, :] = nt(g_row[part, :], l_band[...])
-
-    left.end()
+        out_left[part, :] = decay_rate * state_l[part, :] + gain * nt(g_row[part, :], l_band[...])
+
     for ring in m_rings:
         ring.got()
-
     p_swap = []
-    for k in range(2):
-        part = pl.ds(k * HALF, HALF)
+    for k, (lo, hi) in enumerate(spans):
+        part = pl.ds(lo, hi - lo)
+        left.end(k)
         tile = nn(l_row[part, :], m_col[...])
         p_out[part, :] = tile.astype(jnp.bfloat16)
         p_swap.append(send(p_out.at[part, :], p_in.at[part, :], twin))
@@ -364,15 +370,14 @@
 
     for cp in s_y:
         cp.wait_recv()
-    out_right[...] = (
+    out_right[...] = decay_rate * state_r[...] + gain * (
         q_own[y] + s_in[0].astype(jnp.float32) + s_in[1].astype(jnp.float32) + s_in[2].astype(jnp.float32)
     )
 
-    for k in range(2):
-        part = pl.ds(k * HALF, HALF)
+    for k, (lo, hi) in enumerate(spans):
+        part = pl.ds(lo, hi - lo)
         p_swap[k].wait_recv()
         out_pre[part, lanes(1 - rep)] = p_in[part, :].astype(jnp.float32)
-
     for cp in copies:
         cp.wait_send()
     assert len(copies) == N_COPIES, len(copies)
@@ -383,7 +388,7 @@
     bf16, f32 = jnp.bfloat16, jnp.float32
     any_spec = pl.BlockSpec(memory_space=pl.ANY)
     vmem_spec = pl.BlockSpec(memory_space=pltpu.VMEM)
-    update, left_gram, right_gram = pl.pallas_call(
+    update, new_left, new_right = pl.pallas_call(
         kernel,
         name="shampoo",
         out_shape=(
@@ -391,7 +396,7 @@
             jax.ShapeDtypeStruct((FULL, HALF), f32),
             jax.ShapeDtypeStruct((HALF, FULL), f32),
         ),
-        in_specs=[any_spec] * 3,
+        in_specs=[any_spec] * 5,
         out_specs=[vmem_spec] * 3,
         scratch_shapes=[
             pltpu.VMEM((FULL, HALF), bf16),
@@ -409,7 +414,9 @@
             pltpu.VMEM((3, HALF, FULL), bf16),
             pltpu.VMEM((FULL, HALF), bf16),
             pltpu.VMEM((FULL, HALF), bf16),
-            pltpu.SemaphoreType.DMA((3,)),
+            pltpu.VMEM((FULL, HALF), f32),
+            pltpu.VMEM((HALF, FULL), f32),
+            pltpu.SemaphoreType.DMA((5,)),
             pltpu.SemaphoreType.DMA((N_COPIES,)),
             pltpu.SemaphoreType.DMA((N_COPIES,)),
         ],
@@ -417,9 +424,7 @@
             collective_id=0, has_side_effects=True, vmem_limit_bytes=56 * 2**20
         ),
         cost_estimate=pl.CostEstimate(flops=8 * 2**30, bytes_accessed=4 * 2**20, transcendentals=0),
-    )(replica_deltas[0], left_root, right_root)
-    new_left = decay_rate * left_state + (1.0 - decay_rate) / total * left_gram
-    new_right = decay_rate * right_state + (1.0 - decay_rate) / total * right_gram
+    )(replica_deltas[0], left_root, right_root, left_state, right_state)
     new_momentum = momentum_rate * momentum + update
     new_weights = weights - outer_rate * (momentum_rate * new_momentum + update)
     return (new_weights, new_momentum, new_left, new_right)

time: 93.7 us -> 90.5 us (0.966)
  other arithmetic: 5.79 us -> 2.98 us
  Pallas kernels: 86.9 us -> 84.4 us
  local copies, waits for them, and re-layouts: 0.02 us -> 2.04 us
    add x2 -> x0, other arithmetic: 4.1 us -> none  [the longest x1 2.07 us: shards(): new_left = decay_rate * left_state + (1.0 - decay_rate) / total * left_gram]
    pallas_call x1, Pallas kernels: 86.9 us -> 84.4 us  [shards(): pl.pallas_call(kernel, name='shampoo', out_shape=(jax.ShapeDtypeStruct((F...]
    unnamed x10, local copies, waits for them, and re-layouts: 0.02 us -> 2.04 us
    sub x1, other arithmetic: 1.69 us -> 2.98 us  [shards(): new_weights = weights - outer_rate * (momentum_rate * new_momentum + update)]
where the time goes in v4:
time: 90.5 us; the launch traced here: 90.1 us
  Pallas kernels  84.4 us (93%)
  other arithmetic  2.98 us (3%)
  local copies, waits for them, and re-layouts  2.04 us (2%)
    pallas_call x1, Pallas kernels, shards(): pl.pallas_call(kernel, name='shampoo', out_shape=(jax.ShapeDtypeStruct((F...  84.4 us
    sub x1, other arithmetic, shards(): new_weights = weights - outer_rate * (momentum_rate * new_momentum + update)  2.98 us
    unnamed x10, local copies, waits for them, and re-layouts  2.04 us

profile of v4, /device:TPU:0, one launch (start us, length us, event | category | flops | bytes accessed | tf_op | source)
XLA Modules:
  0.0 90.1 jit_solution(16394867997451665823)
XLA Ops:
  0.6 0.0 copy-start
  0.6 0.0 copy-start.1
  0.7 84.4 %shampoo.1 = (f32[512,512]{1,0:T(8,128)}, f32[512,256]{1,0:T(8,128)}, f32[256,512]{1,0:T(8,128)}) custom-call(bf16[512,512]{1,0:T(8,128)(2,1)} %bitcast.1, bf16[512,256]{1,0:T(8,128)(2,1)} %left_root.1, bf16[256,512]{1,0:T(8,128)(2,1)} %right_root.1, f32[512,256]{1,0:T(8,128)} %left_state.1, f32[256,512]{1,0:T(8,128)} %right_state.1), custom_call_target="tpu_custom_call" | custom-call | flops 8589934592 | bytes 4194304 | tf_op jit(solution)/shard_map/shampoo/pallas_call | solution.py:391
  85.0 0.0 copy-done
  85.1 0.0 copy-done.1
  85.1 0.0 copy-start.3
  85.1 3.0 %multiply_subtract_fusion = (f32[512,512]{1,0:T(8,128)}, f32[512,512]{1,0:T(8,128)}) fusion(f32[512,512]{1,0:T(8,128)S(1)} %copy-done, f32[512,512]{1,0:T(8,128)} %get-tuple-element.7, f32[512,512]{1,0:T(8,128)S(1)} %copy-done.1), kind=kLoop, calls=%fused_computation | loop fusion | flops 1572864 | bytes 5242880 | tf_op jit(solution)/shard_map/sub | solution.py:429
  88.1 0.0 copy-done.3
  88.1 0.0 copy-start.2
  88.1 0.8 copy.13
  88.9 0.4 copy-done.2
  89.3 0.8 copy.14
Async XLA Ops:
  0.6 84.4 %copy-start = (f32[512,512]{1,0:T(8,128)S(1)}, f32[512,512]{1,0:T(8,128)}, u32[]{:S(2)}) copy-start(f32[512,512]{1,0:T(8,128)} %param.8) | copy-start | bytes 3145732
  0.6 84.4 %copy-start.1 = (f32[512,512]{1,0:T(8,128)S(1)}, f32[512,512]{1,0:T(8,128)}, u32[]{:S(2)}) copy-start(f32[512,512]{1,0:T(8,128)} %param.9) | copy-start | bytes 3145732
  85.1 3.0 %copy-start.3 = (f32[512,256]{1,0:T(8,128)S(1)}, f32[512,256]{1,0:T(8,128)}, u32[]{:S(2)}) copy-start(f32[512,256]{1,0:T(8,128)} %get-tuple-element.18) | copy-start | bytes 1572868
  88.1 1.2 %copy-start.2 = (f32[256,512]{1,0:T(8,128)S(1)}, f32[256,512]{1,0:T(8,128)}, u32[]{:S(2)}) copy-start(f32[256,512]{1,0:T(8,128)} %get-tuple-element.19) | copy-start | bytes 1572868

commit v5 on v4

--- a/solution.py
+++ b/solution.py
@@ -322,11 +322,14 @@
             q_out[yy, :, pl.ds(HALF * i, HALF)] = tn(other, g_row[:, band[i]]).astype(jnp.bfloat16)
 
     q_swap = send(q_out, q_in, mate)
+    for ring in m_rings:
+        ring.turn(1)
+        ring.turn(-1)
     left.far_x()
     left.turn_rings()
     for ring in m_rings:
-        ring.turn(1)
-        ring.turn(-1)
+        ring.end(1)
+        ring.end(-1)
 
     @pl.loop(0, 4)
     def _(yy):
@@ -343,9 +346,6 @@
         s_out[yy] = total.astype(jnp.bfloat16)
 
     s_y = [send(s_out.at[(y + 4 + d) % 4], s_in.at[n], along_y(d)) for n, d in enumerate((1, -1, 2))]
-    for ring in m_rings:
-        ring.end(1)
-        ring.end(-1)
 
     gain = (1.0 - decay_rate) / g_row.shape[1]
     load_sl.wait()

time: 90.5 us -> 87.6 us (0.968)
  Pallas kernels: 84.4 us -> 81.8 us
    pallas_call x1, Pallas kernels: 84.4 us -> 81.8 us  [shards(): pl.pallas_call(kernel, name='shampoo', out_shape=(jax.ShapeDtypeStruct((F...]
where the time goes in v5:
time: 87.6 us; the launch traced here: 87.5 us
  Pallas kernels  81.8 us (93%)
  other arithmetic  2.98 us (3%)
  local copies, waits for them, and re-layouts  2.04 us (2%)
    pallas_call x1, Pallas kernels, shards(): pl.pallas_call(kernel, name='shampoo', out_shape=(jax.ShapeDtypeStruct((F...  81.8 us
    sub x1, other arithmetic, shards(): new_weights = weights - outer_rate * (momentum_rate * new_momentum + update)  2.98 us
    unnamed x10, local copies, waits for them, and re-layouts  2.04 us

profile of v5, /device:TPU:0, one launch (start us, length us, event | category | flops | bytes accessed | tf_op | source)
XLA Modules:
  0.0 87.5 jit_solution(4263578165606657923)
XLA Ops:
  0.6 0.0 copy-start
  0.6 0.0 copy-start.1
  0.7 81.8 %shampoo.1 = (f32[512,512]{1,0:T(8,128)}, f32[512,256]{1,0:T(8,128)}, f32[256,512]{1,0:T(8,128)}) custom-call(bf16[512,512]{1,0:T(8,128)(2,1)} %bitcast.1, bf16[512,256]{1,0:T(8,128)(2,1)} %left_root.1, bf16[256,512]{1,0:T(8,128)(2,1)} %right_root.1, f32[512,256]{1,0:T(8,128)} %left_state.1, f32[256,512]{1,0:T(8,128)} %right_state.1), custom_call_target="tpu_custom_call" | custom-call | flops 8589934592 | bytes 4194304 | tf_op jit(solution)/shard_map/shampoo/pallas_call | solution.py:391
  82.4 0.0 copy-done
  82.4 0.0 copy-done.1
  82.4 0.0 copy-start.3
  82.4 3.0 %multiply_subtract_fusion = (f32[512,512]{1,0:T(8,128)}, f32[512,512]{1,0:T(8,128)}) fusion(f32[512,512]{1,0:T(8,128)S(1)} %copy-done, f32[512,512]{1,0:T(8,128)} %get-tuple-element.7, f32[512,512]{1,0:T(8,128)S(1)} %copy-done.1), kind=kLoop, calls=%fused_computation | loop fusion | flops 1572864 | bytes 5242880 | tf_op jit(solution)/shard_map/sub | solution.py:429
  85.4 0.0 copy-done.3
  85.4 0.0 copy-start.2
  85.4 0.8 copy.13
  86.2 0.4 copy-done.2
  86.7 0.8 copy.14
Async XLA Ops:
  0.6 81.8 %copy-start = (f32[512,512]{1,0:T(8,128)S(1)}, f32[512,512]{1,0:T(8,128)}, u32[]{:S(2)}) copy-start(f32[512,512]{1,0:T(8,128)} %param.8) | copy-start | bytes 3145732
  0.6 81.8 %copy-start.1 = (f32[512,512]{1,0:T(8,128)S(1)}, f32[512,512]{1,0:T(8,128)}, u32[]{:S(2)}) copy-start(f32[512,512]{1,0:T(8,128)} %param.9) | copy-start | bytes 3145732
  82.4 3.0 %copy-start.3 = (f32[512,256]{1,0:T(8,128)S(1)}, f32[512,256]{1,0:T(8,128)}, u32[]{:S(2)}) copy-start(f32[512,256]{1,0:T(8,128)} %get-tuple-element.18) | copy-start | bytes 1572868
  85.4 1.2 %copy-start.2 = (f32[256,512]{1,0:T(8,128)S(1)}, f32[256,512]{1,0:T(8,128)}, u32[]{:S(2)}) copy-start(f32[256,512]{1,0:T(8,128)} %get-tuple-element.19) | copy-start | bytes 1572868

commit v6 on v5

--- a/solution.py
+++ b/solution.py
@@ -302,6 +302,9 @@
 
         return refs
 
+    left.turn_x(1)
+    left.near_x()
+    left.turn_x(0)
     m_rings = []
     for k, (lo, hi) in enumerate(spans):
         grad.end(k)
@@ -309,9 +312,6 @@
         m_col[pl.ds(pl.multiple_of(base + lo, 16), hi - lo), :] = tile.astype(jnp.bfloat16)
         m_rings.append(Ring(along_y, y, m_part(k), halves, share=True))
 
-    left.turn_x(1)
-    left.near_x()
-    left.turn_x(0)
 
     band = [lanes(4 * z + xl), lanes(4 * z + 2 + xl)]
 
@@ -325,18 +325,18 @@
     for ring in m_rings:
         ring.turn(1)
         ring.turn(-1)
+    @pl.loop(0, 4)
+    def _(yy):
+        mine = g_row[:, lanes(4 * yy + 2 * h + rep)]
+        for i in range(2):
+            q_own[yy, :, pl.ds(HALF * i, HALF)] = tn(mine, g_row[:, band[i]])
+
     left.far_x()
     left.turn_rings()
     for ring in m_rings:
         ring.end(1)
         ring.end(-1)
 
-    @pl.loop(0, 4)
-    def _(yy):
-        mine = g_row[:, lanes(4 * yy + 2 * h + rep)]
-        for i in range(2):
-            q_own[yy, :, pl.ds(HALF * i, HALF)] = tn(mine, g_row[:, band[i]])
-
     q_swap.wait_recv()
 
     @pl.loop(0, 4)
@@ -346,16 +346,6 @@
         s_out[yy] = total.astype(jnp.bfloat16)
 
     s_y = [send(s_out.at[(y + 4 + d) % 4], s_in.at[n], along_y(d)) for n, d in enumerate((1, -1, 2))]
-
-    gain = (1.0 - decay_rate) / g_row.shape[1]
-    load_sl.wait()
-    load_sr.wait()
-    b_ring.got()
-
-    @pl.loop(0, 2)
-    def _(i):
-        part = pl.ds(pl.multiple_of(i * HALF, HALF), HALF)
-        out_left[part, :] = decay_rate * state_l[part, :] + gain * nt(g_row[part, :], l_band[...])
 
     for ring in m_rings:
         ring.got()
@@ -367,6 +357,16 @@
         p_out[part, :] = tile.astype(jnp.bfloat16)
         p_swap.append(send(p_out.at[part, :], p_in.at[part, :], twin))
         out_pre[part, lanes(rep)] = tile
+
+    gain = (1.0 - decay_rate) / g_row.shape[1]
+    load_sl.wait()
+    load_sr.wait()
+    b_ring.got()
+
+    @pl.loop(0, 2)
+    def _(i):
+        part = pl.ds(pl.multiple_of(i * HALF, HALF), HALF)
+        out_left[part, :] = decay_rate * state_l[part, :] + gain * nt(g_row[part, :], l_band[...])
 
     for cp in s_y:
         cp.wait_recv()

time: 87.6 us -> 86.9 us (level)
  no operation moved by 1% of the time
where the time goes in v6:
time: 86.9 us; the launch traced here: 86.7 us
  Pallas kernels  81 us (93%)
  other arithmetic  2.98 us (3%)
  local copies, waits for them, and re-layouts  2.04 us (2%)
    pallas_call x1, Pallas kernels, shards(): pl.pallas_call(kernel, name='shampoo', out_shape=(jax.ShapeDtypeStruct((F...  81 us
    sub x1, other arithmetic, shards(): new_weights = weights - outer_rate * (momentum_rate * new_momentum + update)  2.98 us
    unnamed x10, local copies, waits for them, and re-layouts  2.04 us

profile of v6, /device:TPU:0, one launch (start us, length us, event | category | flops | bytes accessed | tf_op | source)
XLA Modules:
  0.0 86.7 jit_solution(6064989197313828623)
XLA Ops:
  0.6 0.0 copy-start
  0.6 0.0 copy-start.1
  0.7 81.0 %shampoo.1 = (f32[512,512]{1,0:T(8,128)}, f32[512,256]{1,0:T(8,128)}, f32[256,512]{1,0:T(8,128)}) custom-call(bf16[512,512]{1,0:T(8,128)(2,1)} %bitcast.1, bf16[512,256]{1,0:T(8,128)(2,1)} %left_root.1, bf16[256,512]{1,0:T(8,128)(2,1)} %right_root.1, f32[512,256]{1,0:T(8,128)} %left_state.1, f32[256,512]{1,0:T(8,128)} %right_state.1), custom_call_target="tpu_custom_call" | custom-call | flops 8589934592 | bytes 4194304 | tf_op jit(solution)/shard_map/shampoo/pallas_call | solution.py:391
  81.7 0.0 copy-done
  81.7 0.0 copy-done.1
  81.7 0.0 copy-start.3
  81.7 3.0 %multiply_subtract_fusion = (f32[512,512]{1,0:T(8,128)}, f32[512,512]{1,0:T(8,128)}) fusion(f32[512,512]{1,0:T(8,128)S(1)} %copy-done, f32[512,512]{1,0:T(8,128)} %get-tuple-element.7, f32[512,512]{1,0:T(8,128)S(1)} %copy-done.1), kind=kLoop, calls=%fused_computation | loop fusion | flops 1572864 | bytes 5242880 | tf_op jit(solution)/shard_map/sub | solution.py:429
  84.7 0.0 copy-done.3
  84.7 0.0 copy-start.2
  84.7 0.8 copy.13
  85.5 0.4 copy-done.2
  85.9 0.8 copy.14
Async XLA Ops:
  0.6 81.0 %copy-start = (f32[512,512]{1,0:T(8,128)S(1)}, f32[512,512]{1,0:T(8,128)}, u32[]{:S(2)}) copy-start(f32[512,512]{1,0:T(8,128)} %param.8) | copy-start | bytes 3145732
  0.6 81.0 %copy-start.1 = (f32[512,512]{1,0:T(8,128)S(1)}, f32[512,512]{1,0:T(8,128)}, u32[]{:S(2)}) copy-start(f32[512,512]{1,0:T(8,128)} %param.9) | copy-start | bytes 3145732
  81.7 3.0 %copy-start.3 = (f32[512,256]{1,0:T(8,128)S(1)}, f32[512,256]{1,0:T(8,128)}, u32[]{:S(2)}) copy-start(f32[512,256]{1,0:T(8,128)} %get-tuple-element.18) | copy-start | bytes 1572868
  84.7 1.2 %copy-start.2 = (f32[256,512]{1,0:T(8,128)S(1)}, f32[256,512]{1,0:T(8,128)}, u32[]{:S(2)}) copy-start(f32[256,512]{1,0:T(8,128)} %get-tuple-element.19) | copy-start | bytes 1572868

commit v7 on v6

--- a/solution.py
+++ b/solution.py
@@ -218,6 +218,7 @@
         ).astype(jnp.bfloat16)
         grad.start_z(k)
         grad.start_x(k)
+    r_swap = send(right_root.at[:, lanes(1 - rep)], r_col.at[own_r], twin)
     spread = {
         d: [
             send(
@@ -228,7 +229,6 @@
         ]
         for d in (1, 3, 2)
     }
-    r_swap = send(right_root.at[:, lanes(1 - rep)], r_col.at[own_r], twin)
     left.turn_z(0)
     left.turn_z(1)
 

time: 86.9 us -> 86.9 us (level)
  no operation moved by 1% of the time
where the time goes in v7:
time: 86.9 us; the launch traced here: 86.7 us
  Pallas kernels  81 us (93%)
  other arithmetic  2.98 us (3%)
  local copies, waits for them, and re-layouts  2.04 us (2%)
    pallas_call x1, Pallas kernels, shards(): pl.pallas_call(kernel, name='shampoo', out_shape=(jax.ShapeDtypeStruct((F...  81 us
    sub x1, other arithmetic, shards(): new_weights = weights - outer_rate * (momentum_rate * new_momentum + update)  2.98 us
    unnamed x10, local copies, waits for them, and re-layouts  2.04 us

profile of v7, /device:TPU:0, one launch (start us, length us, event | category | flops | bytes accessed | tf_op | source)
XLA Modules:
  0.0 86.7 jit_solution(3293915026972019229)
XLA Ops:
  0.6 0.0 copy-start
  0.6 0.0 copy-start.1
  0.7 81.0 %shampoo.1 = (f32[512,512]{1,0:T(8,128)}, f32[512,256]{1,0:T(8,128)}, f32[256,512]{1,0:T(8,128)}) custom-call(bf16[512,512]{1,0:T(8,128)(2,1)} %bitcast.1, bf16[512,256]{1,0:T(8,128)(2,1)} %left_root.1, bf16[256,512]{1,0:T(8,128)(2,1)} %right_root.1, f32[512,256]{1,0:T(8,128)} %left_state.1, f32[256,512]{1,0:T(8,128)} %right_state.1), custom_call_target="tpu_custom_call" | custom-call | flops 8589934592 | bytes 4194304 | tf_op jit(solution)/shard_map/shampoo/pallas_call | solution.py:391
  81.7 0.0 copy-done
  81.7 0.0 copy-done.1
  81.7 0.0 copy-start.3
  81.7 3.0 %multiply_subtract_fusion = (f32[512,512]{1,0:T(8,128)}, f32[512,512]{1,0:T(8,128)}) fusion(f32[512,512]{1,0:T(8,128)S(1)} %copy-done, f32[512,512]{1,0:T(8,128)} %get-tuple-element.7, f32[512,512]{1,0:T(8,128)S(1)} %copy-done.1), kind=kLoop, calls=%fused_computation | loop fusion | flops 1572864 | bytes 5242880 | tf_op jit(solution)/shard_map/sub | solution.py:429
  84.7 0.0 copy-done.3
  84.7 0.0 copy-start.2
  84.7 0.8 copy.13
  85.5 0.4 copy-done.2
  85.9 0.8 copy.14
Async XLA Ops:
  0.6 81.0 %copy-start = (f32[512,512]{1,0:T(8,128)S(1)}, f32[512,512]{1,0:T(8,128)}, u32[]{:S(2)}) copy-start(f32[512,512]{1,0:T(8,128)} %param.8) | copy-start | bytes 3145732
  0.6 81.0 %copy-start.1 = (f32[512,512]{1,0:T(8,128)S(1)}, f32[512,512]{1,0:T(8,128)}, u32[]{:S(2)}) copy-start(f32[512,512]{1,0:T(8,128)} %param.9) | copy-start | bytes 3145732
  81.7 3.0 %copy-start.3 = (f32[512,256]{1,0:T(8,128)S(1)}, f32[512,256]{1,0:T(8,128)}, u32[]{:S(2)}) copy-start(f32[512,256]{1,0:T(8,128)} %get-tuple-element.18) | copy-start | bytes 1572868
  84.7 1.2 %copy-start.2 = (f32[256,512]{1,0:T(8,128)S(1)}, f32[256,512]{1,0:T(8,128)}, u32[]{:S(2)}) copy-start(f32[256,512]{1,0:T(8,128)} %get-tuple-element.19) | copy-start | bytes 1572868
